TPU v7x, 128 devices: a whole 4x4x4 slice. The times are simulated.
128 devices in a mesh: batch: 32 (over y, z_hi, x), feat: 4 (over z_lo, core).
Axes of the slice: x: 4, y: 4, z: 4 (z_hi: 2, z_lo: 2; z = z_hi * 2 + z_lo), core: 2. Of those that a mesh axis runs over, the one named last changes fastest.
Arguments:
- view_a: bfloat16 [16384, 4096], P('batch', 'feat')
- view_b: bfloat16 [16384, 4096], P('batch', 'feat')
Outputs:
- grad_a: float32 [16384, 4096], P('batch', 'feat')
- grad_b: float32 [16384, 4096], P('batch', 'feat')
- loss: float32 [], replicated
All inputs are finite; a program needn't handle non-finite values.
Results may differ from a plain program's by a relative error of at most 0.019.
Values may be sent and summed in bfloat16 or wider, within the bound.
A program may use at most 128 MiB of HBM per device.

v0:
```python
import jax
import jax.numpy as jnp
from jax import lax
from jax.sharding import PartitionSpec as P

lam_off = 0.0051
eps_norm = 1e-05


def back_norm(back, normed, inv_v, sum_back, sum_prod, total):
    nfloat = normed.astype(jnp.float32)
    return inv_v * (back - sum_back / total - nfloat * (sum_prod / total))


def shards(view_a, view_b):
    rows = view_a.shape[0]
    feat_block = view_a.shape[1]
    total = rows * lax.axis_size("batch")
    width = feat_block * lax.axis_size("feat")
    tile_rows = width // lax.axis_size("batch")
    values_a = view_a.astype(jnp.float32)
    values_b = view_b.astype(jnp.float32)
    sum_a, sum_b = lax.psum((jnp.sum(values_a, axis=0), jnp.sum(values_b, axis=0)), "batch")
    mean_a = sum_a / total
    mean_b = sum_b / total
    dev_a, dev_b = lax.psum(
        (jnp.sum((values_a - mean_a) ** 2, axis=0), jnp.sum((values_b - mean_b) ** 2, axis=0)),
        "batch",
    )
    var_a = dev_a / total
    var_b = dev_b / total
    inv_a = 1.0 / jnp.sqrt(var_a + eps_norm)
    inv_b = 1.0 / jnp.sqrt(var_b + eps_norm)
    norm_a = ((values_a - mean_a) * inv_a).astype(jnp.bfloat16)
    norm_b = ((values_b - mean_b) * inv_b).astype(jnp.bfloat16)
    norm_b_full = lax.all_gather(norm_b, "feat", axis=1, tiled=True)
    columns = norm_b_full
    corr_tile = (
        lax.psum_scatter(
            lax.dot_general(
                columns, norm_a, (((0,), (0,)), ((), ())), preferred_element_type=jnp.float32
            ),
            "batch",
            scatter_dimension=0,
            tiled=True,
        )
        / total
    )
    second_idx = lax.axis_index("batch") * tile_rows + lax.broadcasted_iota(
        jnp.int32, (tile_rows, feat_block), 0
    )
    first_idx = lax.axis_index("feat") * feat_block + lax.broadcasted_iota(
        jnp.int32, (tile_rows, feat_block), 1
    )
    on_diag = second_idx == first_idx
    local_loss = jnp.sum(
        jnp.where(on_diag, (1.0 - corr_tile) ** 2, lam_off * corr_tile * corr_tile)
    )
    grad_tile = jnp.where(on_diag, -2.0 * (1.0 - corr_tile), 2.0 * lam_off * corr_tile).astype(
        jnp.bfloat16
    )
    piece = lax.all_gather(grad_tile, "batch", axis=0, tiled=True)
    columns = norm_b_full
    back_a = jnp.dot(columns, piece, preferred_element_type=jnp.float32)
    update = lax.dot_general(
        norm_a, piece, (((1,), (1,)), ((), ())), preferred_element_type=jnp.float32
    )
    partial_b = update
    back_a, partial_b = (back_a, partial_b)
    back_b = lax.psum_scatter(partial_b, "feat", scatter_dimension=1, tiled=True)
    float_a = norm_a.astype(jnp.float32)
    float_b = norm_b.astype(jnp.float32)
    sba, spa, sbb, spb = lax.psum(
        (
            jnp.sum(back_a, axis=0),
            jnp.sum(back_a * float_a, axis=0),
            jnp.sum(back_b, axis=0),
            jnp.sum(back_b * float_b, axis=0),
        ),
        "batch",
    )
    grad_a = back_norm(back_a, norm_a, inv_a, sba, spa, total)
    grad_b = back_norm(back_b, norm_b, inv_b, sbb, spb, total)
    loss = lax.psum(local_loss, ("batch", "feat"))
    return (grad_a, grad_b, loss)


def solution(mesh):
    return jax.shard_map(
        shards,
        mesh=mesh,
        in_specs=(P("batch", "feat"), P("batch", "feat")),
        out_specs=(P("batch", "feat"), P("batch", "feat"), P()),
        check_vma=False,
    )
```

profile of v0, /device:TPU:0, one launch (start us, length us, event | category | flops | bytes accessed | tf_op | source)
XLA Modules:
  0.0 869.5 jit_solution(229325512754730310)
XLA Ops:
  7.2 0.0 copy-start
  7.2 0.0 copy-start.1
  7.2 0.0 all-gather.3.cloned.1.call-start
  7.2 1.5 convert_reduce_fusion
  8.8 1.4 convert_reduce_fusion.1
  10.2 98.5 %all-reduce.2 = (f32[1024]{0:T(1024)S(1)}, f32[1024]{0:T(1024)S(1)}) all-reduce(f32[1024]{0:T(1024)S(1)} %convert_reduce_fusion, f32[1024]{0:T(1024)S(1)} %convert_reduce_fusion.1), channel_id=1, replica_groups=mesh['batch'=32,'feat'=4] {'batch'}, use_global_device_ids=true, to_apply=%region_5.0 | all-reduce | flops 2048 | bytes 16384 | tf_op jit(solution)/shard_map/psum | solution.py:23
  108.7 0.0 copy-done
  108.7 0.3 fusion.4
  109.0 0.0 copy-done.1
  109.0 0.3 fusion.6
  109.3 90.0 %all-reduce.1 = (f32[1024]{0:T(1024)S(1)}, f32[1024]{0:T(1024)S(1)}) all-reduce(f32[1024]{0:T(1024)S(1)} %fusion.4, f32[1024]{0:T(1024)S(1)} %fusion.6), channel_id=1, replica_groups=mesh['batch'=32,'feat'=4] {'batch'}, use_global_device_ids=true, to_apply=%region_7.0 | all-reduce | flops 2048 | bytes 16384 | tf_op jit(solution)/shard_map/psum | solution.py:26
  199.3 1.3 fusion.5
  200.6 0.0 all-gather.3.cloned.1.call-update
  200.6 0.0 reduce-scatter.3.cloned.1.call-start
  200.6 41.8 %all-gather.3.cloned.1.call-done = bf16[512,4096]{1,0:T(8,128)(2,1)} async-done(((bf16[512,1024]{1,0:T(8,128)(2,1)}), bf16[512,4096]{1,0:T(8,128)(2,1)}) %all-gather.3.cloned.1.call-update) | async-done | bytes 4194320 | tf_op jit(solution)/shard_map/all_gather | solution.py:36
  242.4 10.4 %fusion.18 = f32[4096,1024]{1,0:T(8,128)} fusion(bf16[512,4096]{1,0:T(8,128)(2,1)} %all-gather.3.cloned.1.call-done, bf16[512,1024]{1,0:T(8,128)(2,1)S(1)} %copy-done.1, f32[1024]{0:T(1024)S(1)} %add_rsqrt_fusion.1, f32[1024]{0:T(1024)S(1)} %get-tuple-element.19), kind=kOutput, calls=%fused_computation.27 | convolution fusion | flops 4297064448 | bytes 22028288 | tf_op jit(solution)/shard_map/dot_general | solution.py:40
  252.8 0.0 reduce-scatter.3.cloned.1.call-update
  252.8 0.0 all-gather.5.cloned.1.call-start
  252.9 224.6 %reduce-scatter.3.cloned.1.call-done = f32[128,1024]{1,0:T(8,128)} async-done(((f32[4096,1024]{1,0:T(8,128)}), f32[128,1024]{1,0:T(8,128)}) %reduce-scatter.3.cloned.1.call-update) | async-done | bytes 524304 | tf_op jit(solution)/shard_map/reduce_scatter | solution.py:39
  477.6 2.6 fusion.15
  480.2 0.0 all-gather.5.cloned.1.call-update
  480.2 0.0 reduce-scatter.5.cloned.1.call-start
  480.3 103.9 %all-gather.5.cloned.1.call-done = bf16[4096,1024]{1,0:T(8,128)(2,1)} async-done(((bf16[128,1024]{1,0:T(8,128)(2,1)}), bf16[4096,1024]{1,0:T(8,128)(2,1)}) %all-gather.5.cloned.1.call-update) | async-done | bytes 8388624 | tf_op jit(solution)/shard_map/all_gather | solution.py:62
  584.1 10.1 %fusion.16 = f32[512,4096]{1,0:T(8,128)} fusion(bf16[4096,1024]{1,0:T(8,128)(2,1)} %all-gather.5.cloned.1.call-done, bf16[512,1024]{1,0:T(8,128)(2,1)S(1)} %copy-done.1, f32[1024]{0:T(1024)S(1)} %add_rsqrt_fusion.1, f32[1024]{0:T(1024)S(1)} %get-tuple-element.19), kind=kOutput, calls=%fused_computation.26 | convolution fusion | flops 4297064448 | bytes 17833984 | tf_op jit(solution)/shard_map/dot_general | solution.py:65
  594.2 0.0 reduce-scatter.5.cloned.1.call-update
  594.2 64.4 %psum.71 = f32[]{:T(128)} all-reduce(f32[]{:T(128)} %get-tuple-element.15), channel_id=1, replica_groups=mesh['batch'=32,'feat'=4] {'batch','feat'}, use_global_device_ids=true, to_apply=%region_19.20 | all-reduce | flops 1 | bytes 8 | tf_op jit(solution)/shard_map/psum | solution.py:84
  658.7 10.6 %fusion.21 = (f32[1024]{0:T(1024)S(1)}, f32[1024]{0:T(1024)S(1)}, f32[512,1024]{1,0:T(8,128)}) fusion(f32[1024]{0:T(1024)S(1)} %add_rsqrt_fusion.1, f32[1024]{0:T(1024)S(1)} %get-tuple-element.19, bf16[512,1024]{1,0:T(8,128)(2,1)S(1)} %copy-done.1, bf16[512,4096]{1,0:T(8,128)(2,1)} %all-gather.3.cloned.1.call-done, ...), kind=kOutput, calls=%fused_computation.39 | convolution fusion | flops 4299159552 | bytes 15745024 | tf_op jit(solution)/shard_map/dot_general | solution.py:64
  669.3 3.2 reduce-scatter.5.cloned.1.call-done
  672.5 2.0 fusion.20
  674.5 183.0 %all-reduce = (f32[1024]{0:T(1024)S(1)}, f32[1024]{0:T(1024)S(1)}, f32[1024]{0:T(1024)S(1)}, f32[1024]{0:T(1024)S(1)}) all-reduce(f32[1024]{0:T(1024)S(1)} %get-tuple-element.6, f32[1024]{0:T(1024)S(1)} %get-tuple-element.5, f32[1024]{0:T(1024)S(1)} %get-tuple-element.4, ...), channel_id=1, replica_groups=mesh['batch'=32,'feat'=4] {'batch'}, use_global_device_ids=true, to_apply=%region_12.13 | all-reduce | flops 4096 | bytes 32768 | tf_op jit(solution)/shard_map/psum | solution.py:73
  857.6 0.0 copy-start.2
  857.6 3.6 fusion.10
  861.2 0.0 copy-done.2
  861.2 1.8 fusion.13
  (9 shorter events, 0.0 us)
Async XLA Ops:
  7.2 101.5 %copy-start = (bf16[512,1024]{1,0:T(8,128)(2,1)S(1)}, bf16[512,1024]{1,0:T(8,128)(2,1)}, u32[]{:S(2)}) copy-start(bf16[512,1024]{1,0:T(8,128)(2,1)} %param.3) | copy-start | bytes 3145732
  7.2 101.8 %copy-start.1 = (bf16[512,1024]{1,0:T(8,128)(2,1)S(1)}, bf16[512,1024]{1,0:T(8,128)(2,1)}, u32[]{:S(2)}) copy-start(bf16[512,1024]{1,0:T(8,128)(2,1)} %param.2) | copy-start | bytes 3145732
  7.2 235.2 %all-gather.3.cloned.1.call-start = ((), (), s32[]{:S(2)}) async-start(), calls=%async_computation.2 | async-start | bytes 5242880 | tf_op jit(solution)/shard_map/all_gather | solution.py:36
  200.6 277.0 %reduce-scatter.3.cloned.1.call-start = ((), (), s32[]{:S(2)}) async-start(), calls=%async_computation.3 | async-start | bytes 17301504 | tf_op jit(solution)/shard_map/reduce_scatter | solution.py:39
  252.8 331.3 %all-gather.5.cloned.1.call-start = ((), (), s32[]{:S(2)}) async-start(), calls=%async_computation.4 | async-start | bytes 8650752 | tf_op jit(solution)/shard_map/all_gather | solution.py:62
  480.2 192.3 %reduce-scatter.5.cloned.1.call-start = ((), (), s32[]{:S(2)}) async-start(), calls=%async_computation.5 | async-start | bytes 10485760 | tf_op jit(solution)/shard_map/reduce_scatter | solution.py:70
  857.6 3.6 copy-start.2
Sparse Core Ops, SparseCore 0:
  200.7 41.6 all-gather.2
  253.0 224.5 reduce-scatter.2
  481.2 102.8 all-gather.4
  594.4 78.0 reduce-scatter.4
where the time goes:
time: 870 us
  blocking collectives  436 us (50%)
  waiting for transfers between devices  374 us (43%)
  matrix products  31.1 us (4%)
  other arithmetic  15 us (2%)
  between operations  13.9 us (2%)
    reduce_scatter x1, waiting for transfers between devices, shards(): lax.psum_scatter(lax.dot_general(columns, norm_a, (((0,), (0,)), ((), ())...  225 us
    psum x1, blocking collectives, shards(): lax.psum((jnp.sum(back_a, axis=0), jnp.sum(back_a * float_a, axis=0), jnp...  183 us
    all_gather x1, waiting for transfers between devices, shards(): piece = lax.all_gather(grad_tile, 'batch', axis=0, tiled=True)  104 us
    psum x1, blocking collectives, shards(): lax.psum((jnp.sum(values_a, axis=0), jnp.sum(values_b, axis=0)), 'batch')  98.5 us
    psum x1, blocking collectives, shards(): lax.psum((jnp.sum((values_a - mean_a) ** 2, axis=0), jnp.sum((values_b -...  90 us
    psum x1, blocking collectives, shards(): loss = lax.psum(local_loss, ('batch', 'feat'))  64.4 us
    all_gather x1, waiting for transfers between devices, shards(): norm_b_full = lax.all_gather(norm_b, 'feat', axis=1, tiled=True)  41.8 us
  transfers between devices with their start and end apart: 4, of which 4 were waited for; matrix products, arithmetic and copies ran while one was open for 1% of the time, Pallas kernels for 0%

commit v1 on v0

v1 whole, which is shorter than its diff:
```python
import functools

import jax
import jax.numpy as jnp
from jax import lax
from jax.experimental import pallas as pl
from jax.experimental.pallas import tpu as pltpu
from jax.sharding import PartitionSpec as P

lam_off = 0.0051
eps_norm = 1e-05
f32 = jnp.float32
bf16 = jnp.bfloat16
MESH = pl.DeviceIdType.MESH

ROWS = 512
FB = 1024
W = 1024
CPK = FB // W
NCH = 4 * CPK
TOTAL = 16384


def column_sum(fn, rows, step=32):
    def body(i, acc):
        v = fn(pl.ds(pl.multiple_of(i * step, step), step))
        return acc + jnp.sum(v.reshape(step // 8, 8, v.shape[-1]), axis=0)

    acc = lax.fori_loop(0, rows // step, body, jnp.zeros((8, FB), f32))
    return jnp.sum(acc, axis=0, keepdims=True)


def kernel(
    a_ref, b_ref, ga_ref, gb_ref, loss_ref,
    na, nat, bn, braw, sb, ld1, sb2, ld2, ub, zl_buf, gt, pbs, pbl,
    ex_x, ex_y, ex_z, lo_x, lo_y, lo_f, vec, lacc,
    ss1, rs1, ss2, rs2, ssz, rsz, ssg2, rsg2, ssg1, rsg1, ssb, rsb, ssp, rsp,
    sse, rse, ssl, rsl,
):
    bi = lax.axis_index("batch")
    fi = lax.axis_index("feat")
    y, zh, x = bi // 8, (bi // 4) % 2, bi % 4
    zl, core = fi // 2, fi % 2

    def dev(y_, zh_, x_, zl_, c_):
        return (((y_ + 4) % 4) * 8 + zh_ * 4 + ((x_ + 4) % 4), zl_ * 2 + c_)

    xdev = {d: dev(y, zh, x + d, zl, core) for d in (1, 2, 3)}
    ydev = {d: dev(y + d, zh, x, zl, core) for d in (1, 2, 3)}
    zhdev = dev(y, 1 - zh, x, zl, core)
    fdev = {1: dev(y, zh, x, zl, 1 - core), 2: dev(y, zh, x, 1 - zl, core),
            3: dev(y, zh, x, 1 - zl, 1 - core)}

    bar = pltpu.get_barrier_semaphore()
    partners = list(xdev.values()) + list(ydev.values()) + [zhdev] + list(fdev.values())
    for q in partners:
        pl.semaphore_signal(bar, inc=1, device_id=q, device_id_type=MESH)
    pl.semaphore_wait(bar, len(partners))

    pending = []

    def send(src, dst, s, r, to):
        cp = pltpu.make_async_remote_copy(
            src_ref=src, dst_ref=dst, send_sem=s, recv_sem=r, device_id=to, device_id_type=MESH)
        cp.start()
        pending.append(cp)

    def arrived(region, s, r):
        pltpu.make_async_remote_copy(
            src_ref=region, dst_ref=region, send_sem=s, recv_sem=r, device_id=zhdev,
            device_id_type=MESH).wait_recv()

    NB = 2
    RB = ROWS // NB
    for i in range(NB):
        rr = pl.ds(i * RB, RB)
        send(b_ref.at[rr], braw.at[0, rr], ssb.at[0, i], rsb.at[0, i], fdev[1])
        send(b_ref.at[rr], braw.at[1, rr], ssb.at[1, i], rsb.at[1, i], fdev[2])

    def forward_raw():
        for i in range(NB):
            rr = pl.ds(i * RB, RB)
            arrived(braw.at[1, rr], ssb.at[1, i], rsb.at[1, i])
            send(braw.at[1, rr], braw.at[2, rr], ssb.at[2, i], rsb.at[2, i], fdev[1])

    def raw_arrived(k):
        if k in (1, 3):
            for i in range(NB):
                rr = pl.ds(i * RB, RB)
                arrived(braw.at[k - 1, rr], ssb.at[k - 1, i], rsb.at[k - 1, i])

    def stage_send(buf, me, peers, base, s, r):
        for i, to in enumerate(peers):
            send(buf.at[me], buf.at[me], s.at[base + i], r.at[base + i], to)

    def stage_wait(buf, froms, base, s, r):
        for i, q in enumerate(froms):
            arrived(buf.at[q], s.at[base + i], r.at[base + i])

    xfrom = [(x + 4 - d) % 4 for d in (1, 2, 3)]
    yfrom = [(y + 4 - d) % 4 for d in (1, 2, 3)]
    xto = [xdev[d] for d in (1, 2, 3)]
    yto = [ydev[d] for d in (1, 2, 3)]

    def ex_parts(e):
        bx, by, bz = ex_x.at[e], ex_y.at[e], ex_z.at[e]
        s, r = sse.at[e], rse.at[e]
        return bx, by, bz, s, r

    def ex_start(e, value):
        bx, by, bz, s, r = ex_parts(e)
        bx[x] = value
        stage_send(bx, x, xto, 0, s, r)

    def ex_mid(e, merge):
        bx, by, bz, s, r = ex_parts(e)
        stage_wait(bx, xfrom, 0, s, r)
        by[y] = merge([bx[q] for q in range(4)], ROWS)
        stage_send(by, y, yto, 3, s, r)

    def ex_last(e, merge):
        bx, by, bz, s, r = ex_parts(e)
        stage_wait(by, yfrom, 3, s, r)
        bz[zh] = merge([by[q] for q in range(4)], ROWS * 4)
        stage_send(bz, zh, [zhdev], 6, s, r)

    def ex_end(e, merge):
        bx, by, bz, s, r = ex_parts(e)
        stage_wait(bz, [1 - zh], 6, s, r)
        return merge([bz[0], bz[1]], ROWS * 16)

    def merge_sum(vs, n):
        t = vs[0]
        for v in vs[1:]:
            t = t + v
        return t

    def merge_moments(vs, n):
        mean = merge_sum(vs, n)[0:2] * (1.0 / len(vs))
        m2 = merge_sum(vs, n)[2:4]
        for v in vs:
            d = v[0:2] - mean
            m2 = m2 + float(n) * d * d
        return jnp.concatenate([mean, m2, jnp.zeros((4, FB), f32)], axis=0)

    mean_a = column_sum(lambda s: a_ref[s].astype(f32), ROWS) * (1.0 / ROWS)
    mean_b = column_sum(lambda s: b_ref[s].astype(f32), ROWS) * (1.0 / ROWS)

    def dev2(ref, mean):
        def f(s):
            d = ref[s].astype(f32) - mean
            return d * d
        return column_sum(f, ROWS)

    m2_a = dev2(a_ref, mean_a)
    m2_b = dev2(b_ref, mean_b)
    ex_start(0, jnp.concatenate([mean_a, mean_b, m2_a, m2_b, jnp.zeros((4, FB), f32)], axis=0))
    ex_mid(0, merge_moments)
    ex_last(0, merge_moments)
    st = ex_end(0, merge_moments)
    inv = 1.0 / jnp.sqrt(st[2:4] * (1.0 / TOTAL) + eps_norm)
    vec[0] = jnp.concatenate([st[0:2], inv, jnp.zeros((4, FB), f32)], axis=0)
    for k in (1, 2, 3):
        send(vec.at[0], vec.at[k], ssb.at[3, k - 1], rsb.at[3, k - 1], fdev[k])

    def normalise(src, dst, mean, iv):
        def body(i, _):
            s = pl.ds(pl.multiple_of(i * 64, 64), 64)
            dst[s, :] = ((src[s, :].astype(f32) - mean) * iv).astype(bf16)
            return 0
        lax.fori_loop(0, ROWS // 64, body, 0)

    normalise(a_ref, na, st[0:1], inv[0:1])
    normalise(b_ref, bn.at[0], st[1:2], inv[1:2])
    for i in range(4):
        nat[pl.ds(i * 256, 256), :] = na[:, pl.ds(i * 256, 256)].T
    dsum = column_sum(lambda s: na[s].astype(f32) * bn[0, s].astype(f32), ROWS)
    ex_start(1, jnp.concatenate([dsum, jnp.zeros((7, FB), f32)], axis=0))
    lacc[...] = jnp.zeros_like(lacc)

    def prepare(k):
        if k == 0:
            return
        raw_arrived(k)
        arrived(vec.at[k], ssb.at[3, k - 1], rsb.at[3, k - 1])
        v = vec[k]
        normalise(braw.at[k - 1], bn.at[k], v[1:2], v[3:4])

    p1 = (x, y)
    p2 = (y, x)
    right1, left1 = (xdev[1], ydev[1]), (xdev[3], ydev[3])
    right2, left2 = (ydev[1], xdev[1]), (ydev[3], xdev[3])

    def at(q, d):
        return (q + d) % 4

    def piece(base, q, size, lo, n):
        return pl.ds(pl.multiple_of(base + q * size + lo, 16), n)

    def ring_early(buf, land, base, q, size, right, left, s, r):
        hf = size // 2
        send(buf.at[piece(base, at(q, 2), size, 0, hf)], land.at[0], s.at[0], r.at[0], right)
        send(buf.at[piece(base, at(q, 2), size, hf, hf)], land.at[1], s.at[1], r.at[1], left)
        send(buf.at[piece(base, at(q, 1), size, hf, hf)], land.at[2], s.at[2], r.at[2], right)
        send(buf.at[piece(base, at(q, 3), size, 0, hf)], land.at[3], s.at[3], r.at[3], left)

    def ring_late(buf, land, base, q, size, right, left, s, r):
        hf = size // 2
        ra = piece(base, at(q, 1), size, 0, hf)
        lb = piece(base, at(q, 3), size, hf, hf)
        arrived(land.at[0], s.at[0], r.at[0])
        buf[ra, :] = (buf[ra, :].astype(f32) + land[0].astype(f32)).astype(bf16)
        send(buf.at[ra], land.at[4], s.at[4], r.at[4], right)
        arrived(land.at[1], s.at[1], r.at[1])
        buf[lb, :] = (buf[lb, :].astype(f32) + land[1].astype(f32)).astype(bf16)
        send(buf.at[lb], land.at[5], s.at[5], r.at[5], left)

    def ring_fin(buf, land, base, q, size, out, obase, s, r):
        hf = size // 2
        for m in (2, 3, 4, 5):
            arrived(land.at[m], s.at[m], r.at[m])
        ha = piece(base, q, size, 0, hf)
        hb = piece(base, q, size, hf, hf)
        out[pl.ds(obase, hf), :] = (
            buf[ha, :].astype(f32) + land[3].astype(f32) + land[4].astype(f32)).astype(bf16)
        out[pl.ds(obase + hf, hf), :] = (
            buf[hb, :].astype(f32) + land[2].astype(f32) + land[5].astype(f32)).astype(bf16)

    def gather_early(buf, base, q, size, right, left, s, r):
        own = buf.at[piece(base, q, size, 0, size)]
        send(own, own, s.at[0], r.at[0], right)
        send(own, own, s.at[1], r.at[1], left)

    def gather_late(buf, base, q, size, right, left, s, r):
        hf = size // 2
        fl = buf.at[piece(base, at(q, 3), size, 0, size)]
        fr = buf.at[piece(base, at(q, 1), size, 0, size)]
        arrived(fl, s.at[0], r.at[0])
        ha = buf.at[piece(base, at(q, 3), size, 0, hf)]
        send(ha, ha, s.at[2], r.at[2], right)
        arrived(fr, s.at[1], r.at[1])
        hb = buf.at[piece(base, at(q, 1), size, hf, hf)]
        send(hb, hb, s.at[3], r.at[3], left)

    def gather_fin(buf, base, q, size, s, r):
        hf = size // 2
        arrived(buf.at[piece(base, at(q, 2), size, 0, hf)], s.at[2], r.at[2])
        arrived(buf.at[piece(base, at(q, 2), size, hf, hf)], s.at[3], r.at[3])

    def blk(c):
        return c // CPK

    def col(c):
        return (c % CPK) * W

    def t_dot(c):
        k = blk(c)
        if c % CPK == 0:
            prepare(k)
        n = 256

        def body(j, _):
            o = pl.multiple_of(j * n, n)
            i = pl.multiple_of(col(c) + j * n, n)
            sb[c, :, pl.ds(o, n)] = jnp.dot(
                nat[...], bn[k, :, pl.ds(i, n)], preferred_element_type=f32).astype(bf16)
            return 0

        lax.fori_loop(0, W // n, body, 0)
        for h in (0, 1):
            ring_early(sb.at[c], ld1.at[c, h], 512 * h, p1[h], 128, right1[h], left1[h],
                       ss1.at[c, h], rs1.at[c, h])

    def t_late1(c):
        for h in (0, 1):
            ring_late(sb.at[c], ld1.at[c, h], 512 * h, p1[h], 128, right1[h], left1[h],
                      ss1.at[c, h], rs1.at[c, h])

    def t_fin1(c):
        for h in (0, 1):
            ring_fin(sb.at[c], ld1.at[c, h], 512 * h, p1[h], 128, sb2.at[c, h], 0,
                     ss1.at[c, h], rs1.at[c, h])
            ring_early(sb2.at[c, h], ld2.at[c, h], 0, p2[h], 32, right2[h], left2[h],
                       ss2.at[c, h], rs2.at[c, h])

    def t_late2(c):
        for h in (0, 1):
            ring_late(sb2.at[c, h], ld2.at[c, h], 0, p2[h], 32, right2[h], left2[h],
                      ss2.at[c, h], rs2.at[c, h])

    def t_fin2(c):
        for h in (0, 1):
            ring_fin(sb2.at[c, h], ld2.at[c, h], 0, p2[h], 32, ub.at[c], 32 * h,
                     ss2.at[c, h], rs2.at[c, h])
        send(ub.at[c], zl_buf.at[c], ssz.at[c], rsz.at[c], zhdev)

    def t_tile(c):
        arrived(zl_buf.at[c], ssz.at[c], rsz.at[c])
        for h in (0, 1):
            base = 512 * h + 128 * p1[h] + 32 * p2[h]
            corr = (ub[c, pl.ds(32 * h, 32), :].astype(f32)
                    + zl_buf[c, pl.ds(32 * h, 32), :].astype(f32)) * (1.0 / TOTAL)
            if blk(c) == 0:
                diag = vec[4, 0:1, pl.ds(col(c), W)]
                rows = base + lax.broadcasted_iota(jnp.int32, (32, W), 0)
                cols = col(c) + lax.broadcasted_iota(jnp.int32, (32, W), 1)
                on = rows == cols
                gap = jnp.broadcast_to(1.0 - diag, (32, W))
                l = jnp.where(on, gap * gap, lam_off * corr * corr)
                g = jnp.where(on, -2.0 * gap, 2.0 * lam_off * corr)
            else:
                l = lam_off * corr * corr
                g = 2.0 * lam_off * corr
            lacc[...] += jnp.sum(l.reshape(4, 8, W), axis=0)
            gt[c, pl.ds(pl.multiple_of(base, 32), 32), :] = g.astype(bf16)
        for h in (0, 1):
            gather_early(gt.at[c], 512 * h + 128 * p1[h], p2[h], 32, right2[h], left2[h],
                         ssg2.at[c, h], rsg2.at[c, h])

    def t_fwd2(c):
        for h in (0, 1):
            gather_late(gt.at[c], 512 * h + 128 * p1[h], p2[h], 32, right2[h], left2[h],
                        ssg2.at[c, h], rsg2.at[c, h])

    def t_gat1(c):
        for h in (0, 1):
            gather_fin(gt.at[c], 512 * h + 128 * p1[h], p2[h], 32, ssg2.at[c, h], rsg2.at[c, h])
            gather_early(gt.at[c], 512 * h, p1[h], 128, right1[h], left1[h],
                         ssg1.at[c, h], rsg1.at[c, h])

    def t_fwd1(c):
        for h in (0, 1):
            gather_late(gt.at[c], 512 * h, p1[h], 128, right1[h], left1[h],
                        ssg1.at[c, h], rsg1.at[c, h])

    started = []

    def t_back(c):
        k = blk(c)
        n = 256
        for h in (0, 1):
            gather_fin(gt.at[c], 512 * h, p1[h], 128, ssg1.at[c, h], rsg1.at[c, h])
        first = not started
        started.append(c)

        if c % CPK == 0 and k == 2:
            pass

        def body_b(j, _):
            o = pl.multiple_of(j * n, n)
            i = pl.multiple_of(col(c) + j * n, n)
            v = jnp.dot(na[...], gt[c, :, pl.ds(o, n)], preferred_element_type=f32)
            if k == 0:
                gb_ref[:, pl.ds(i, n)] = v
            elif k == 2:
                pbs[1, :, pl.ds(i, n)] = (
                    v + pbl[2, :, pl.ds(i, n)].astype(f32)).astype(bf16)
            else:
                pbs[k - 1, :, pl.ds(i, n)] = v.astype(bf16)
            return 0

        cs = pl.ds(col(c), W)
        if k == 2:
            arrived(pbl.at[2, :, cs], ssp.at[2, c % CPK], rsp.at[2, c % CPK])
        lax.fori_loop(0, W // n, body_b, 0)
        if k != 0:
            to = fdev[2] if k == 2 else fdev[1]
            send(pbs.at[k - 1, :, cs], pbl.at[k - 1, :, cs],
                 ssp.at[k - 1, c % CPK], rsp.at[k - 1, c % CPK], to)

        def body_a(j, _):
            o = pl.multiple_of(j * n, n)
            v = lax.dot_general(bn[k, :, cs], gt[c, pl.ds(o, n), :], (((1,), (1,)), ((), ())),
                                preferred_element_type=f32)
            if first:
                ga_ref[:, pl.ds(o, n)] = v
            else:
                ga_ref[:, pl.ds(o, n)] += v
            return 0

        lax.fori_loop(0, FB // n, body_a, 0)

    def diag_done():
        d = ex_end(1, merge_sum)
        vec[4] = d * (1.0 / TOTAL)

    def loss_start():
        lo_x[x] = lacc[...]
        stage_send(lo_x, x, xto, 0, ssl, rsl)

    def loss_mid():
        stage_wait(lo_x, xfrom, 0, ssl, rsl)
        lo_y[y] = merge_sum([lo_x[q] for q in range(4)], 0)
        stage_send(lo_y, y, yto, 3, ssl, rsl)

    def loss_feat():
        stage_wait(lo_y, yfrom, 3, ssl, rsl)
        lo_f[fi] = merge_sum([lo_y[q] for q in range(4)], 0)
        stage_send(lo_f, fi, [fdev[1], fdev[2], fdev[3]], 6, ssl, rsl)

    def loss_end():
        stage_wait(lo_f, [fi + 1 - 2 * core, (fi + 2) % 4, (fi + 2) % 4 + 1 - 2 * core], 6, ssl, rsl)
        t = merge_sum([lo_f[q] for q in range(4)], 0)
        loss_ref[...] = jnp.full((8, 128), jnp.sum(t), f32)

    t_dot(0)
    ex_mid(1, merge_sum)
    t_late1(0)
    ex_last(1, merge_sum)
    t_dot(1)
    t_fin1(0)
    diag_done()
    t_late1(1)
    forward_raw()
    t_late2(0)
    t_dot(2)
    t_fin2(0)
    t_fin1(1)
    t_late1(2)
    t_dot(3)
    t_late2(1)
    t_fin1(2)
    t_fin2(1)
    t_late1(3)
    t_late2(2)
    t_fin1(3)
    t_fin2(2)
    t_tile(2)
    t_late2(3)
    t_fwd2(2)
    t_fin2(3)
    t_tile(0)
    t_tile(1)
    t_gat1(2)
    t_tile(3)
    t_fwd1(2)
    t_fwd2(3)
    loss_start()
    t_gat1(3)
    t_fwd2(0)
    t_fwd2(1)
    t_fwd1(3)
    t_gat1(0)
    loss_mid()
    t_gat1(1)
    t_back(3)
    t_fwd1(0)
    t_back(2)
    loss_feat()
    t_fwd1(1)
    t_back(1)
    t_back(0)
    loss_end()

    for j in range(CPK):
        cs = pl.ds(j * W, W)
        arrived(pbl.at[0, :, cs], ssp.at[0, j], rsp.at[0, j])
        arrived(pbl.at[1, :, cs], ssp.at[1, j], rsp.at[1, j])

    def add_b(i, acc):
        s = pl.ds(pl.multiple_of(i * 32, 32), 32)
        v = gb_ref[s, :] + pbl[0, s, :].astype(f32) + pbl[1, s, :].astype(f32)
        gb_ref[s, :] = v
        u = ga_ref[s, :]
        fold = lambda t: jnp.sum(t.reshape(4, 8, FB), axis=0)
        return (acc[0] + fold(u), acc[1] + fold(u * na[s, :].astype(f32)),
                acc[2] + fold(v), acc[3] + fold(v * bn[0, s, :].astype(f32)))

    z8 = jnp.zeros((8, FB), f32)
    acc = lax.fori_loop(0, ROWS // 32, add_b, (z8, z8, z8, z8))
    ex_start(2, jnp.concatenate([jnp.sum(t, axis=0, keepdims=True) for t in acc]
                                + [jnp.zeros((4, FB), f32)], axis=0))
    ex_mid(2, merge_sum)
    ex_last(2, merge_sum)
    m = ex_end(2, merge_sum) * (1.0 / TOTAL)
    iv = vec[0]

    def finish(i, _):
        s = pl.ds(pl.multiple_of(i * 32, 32), 32)
        ga_ref[s, :] = iv[2:3] * (ga_ref[s, :] - m[0:1] - na[s, :].astype(f32) * m[1:2])
        gb_ref[s, :] = iv[3:4] * (gb_ref[s, :] - m[2:3] - bn[0, s, :].astype(f32) * m[3:4])
        return 0

    lax.fori_loop(0, ROWS // 32, finish, 0)
    for cp in pending:
        cp.wait_send()


def shards(view_a, view_b):
    vm = pl.BlockSpec(memory_space=pltpu.VMEM)
    dma = pltpu.SemaphoreType.DMA
    scratch = [
        pltpu.VMEM((ROWS, FB), bf16),
        pltpu.VMEM((FB, ROWS), bf16),
        pltpu.VMEM((4, ROWS, FB), bf16),
        pltpu.VMEM((3, ROWS, FB), bf16),
        pltpu.VMEM((NCH, FB, W), bf16),
        pltpu.VMEM((NCH, 2, 6, 64, W), bf16),
        pltpu.VMEM((NCH, 2, 128, W), bf16),
        pltpu.VMEM((NCH, 2, 6, 16, W), bf16),
        pltpu.VMEM((NCH, 64, W), bf16),
        pltpu.VMEM((NCH, 64, W), bf16),
        pltpu.VMEM((NCH, FB, W), bf16),
        pltpu.VMEM((3, ROWS, FB), bf16),
        pltpu.VMEM((3, ROWS, FB), bf16),
        pltpu.VMEM((3, 4, 8, FB), f32),
        pltpu.VMEM((3, 4, 8, FB), f32),
        pltpu.VMEM((3, 2, 8, FB), f32),
        pltpu.VMEM((4, 8, W), f32),
        pltpu.VMEM((4, 8, W), f32),
        pltpu.VMEM((4, 8, W), f32),
        pltpu.VMEM((5, 8, FB), f32),
        pltpu.VMEM((8, W), f32),
        dma((NCH, 2, 6)), dma((NCH, 2, 6)),
        dma((NCH, 2, 6)), dma((NCH, 2, 6)),
        dma((NCH,)), dma((NCH,)),
        dma((NCH, 2, 4)), dma((NCH, 2, 4)),
        dma((NCH, 2, 4)), dma((NCH, 2, 4)),
        dma((4, 4)), dma((4, 4)),
        dma((3, CPK)), dma((3, CPK)),
        dma((3, 7)), dma((3, 7)),
        dma((9,)), dma((9,)),
    ]
    ga, gb, loss = pl.pallas_call(
        kernel,
        out_shape=(
            jax.ShapeDtypeStruct((ROWS, FB), f32),
            jax.ShapeDtypeStruct((ROWS, FB), f32),
            jax.ShapeDtypeStruct((8, 128), f32),
        ),
        in_specs=[vm, vm],
        out_specs=(vm, vm, vm),
        scratch_shapes=scratch,
        compiler_params=pltpu.CompilerParams(
            collective_id=0, has_side_effects=True, vmem_limit_bytes=60 * 2**20),
        name="barlow",
    )(view_a, view_b)
    return ga, gb, loss[0, 0]


def solution(mesh):
    return jax.shard_map(
        shards,
        mesh=mesh,
        in_specs=(P("batch", "feat"), P("batch", "feat")),
        out_specs=(P("batch", "feat"), P("batch", "feat"), P()),
        check_vma=False,
    )
```

time: 870 us -> 182 us (0.21)
  blocking collectives: 436 us -> 0 us
  waiting for transfers between devices: 374 us -> 0 us
  Pallas kernels: 0 us -> 175 us
  matrix products: 31.1 us -> 0 us
  other arithmetic: 15 us -> 0 us
  between operations: 13.9 us -> 0.64 us
    psum x4 -> x0, blocking collectives: 436 us -> none  [the longest x1 183 us: shards(): lax.psum((jnp.sum(back_a, axis=0), jnp.sum(back_a * float_a, axis=0), jnp...]
    reduce_scatter x2 -> x0, waiting for transfers between devices: 228 us -> none  [the longest x1 225 us: shards(): lax.psum_scatter(lax.dot_general(columns, norm_a, (((0,), (0,)), ((), ())...]
    pallas_call x0 -> x1, Pallas kernels: none -> 175 us  [shards(): pl.pallas_call(kernel, out_shape=(jax.ShapeDtypeStruct((ROWS, FB), f32),...]
    all_gather x2 -> x0, waiting for transfers between devices: 146 us -> none  [the longest x1 104 us: shards(): piece = lax.all_gather(grad_tile, 'batch', axis=0, tiled=True)]
    dot_general x3 -> x0, matrix products: 31.1 us -> none  [the longest x1 10.6 us: shards(): back_a = jnp.dot(columns, piece, preferred_element_type=jnp.float32)]
  transfers between devices with their start and end apart: 4 -> 0, of which waited for: 4 -> 0; matrix products, arithmetic and copies ran while one was open for 1% -> 0% of each run, Pallas kernels for 0% -> 0%
where the time goes in v1:
time: 182 us
  Pallas kernels  175 us (96%)
  local copies, waits for them, and re-layouts  5.82 us (3%)
    pallas_call x1, Pallas kernels, shards(): pl.pallas_call(kernel, out_shape=(jax.ShapeDtypeStruct((ROWS, FB), f32),...  175 us
    unnamed x4, local copies, waits for them, and re-layouts  4.63 us

profile of v1, /device:TPU:0, one launch (start us, length us, event | category | flops | bytes accessed | tf_op | source)
XLA Modules:
  0.0 181.9 jit_solution(16207485315978353108)
XLA Ops:
  0.6 175.5 %barlow.1 = (f32[512,1024]{1,0:T(8,128)}, f32[512,1024]{1,0:T(8,128)}, f32[8,128]{1,0:T(8,128)}) custom-call(bf16[512,1024]{1,0:T(8,128)(2,1)} %a_ref.1, bf16[512,1024]{1,0:T(8,128)(2,1)} %b_ref.1), custom_call_target="tpu_custom_call" | custom-call | tf_op jit(solution)/shard_map/barlow/pallas_call | solution.py:524
  176.1 1.2 slice.3
  177.3 0.0 copy-start
  177.3 3.3 %copy.7 = f32[512,1024]{1,0:T(8,128)} copy(f32[512,1024]{1,0:T(8,128)} %get-tuple-element.12) | data formatting | bytes 4194304
  180.6 0.0 copy-done
  180.6 1.3 copy.8
Async XLA Ops:
  177.3 3.3 %copy-start = (f32[512,1024]{1,0:T(8,128)S(1)}, f32[512,1024]{1,0:T(8,128)}, u32[]{:S(2)}) copy-start(f32[512,1024]{1,0:T(8,128)} %get-tuple-element.13) | copy-start | bytes 6291460

commit v2 on v0

v2 whole, which is shorter than its diff:
```python
import jax
import jax.numpy as jnp
from jax import lax
from jax.experimental import pallas as pl
from jax.experimental.pallas import tpu as pltpu
from jax.sharding import PartitionSpec as P

lam_off = 0.0051
eps_norm = 1e-05
f32 = jnp.float32
bf16 = jnp.bfloat16
MESH = pl.DeviceIdType.MESH

ROWS = 512
RX = ROWS + 16
FB = 1024
CPK = 2
W = FB // CPK
NCH = 4 * CPK
TOTAL = 16384


def column_sum(fn, rows, step=32):
    def body(i, acc):
        v = fn(pl.ds(pl.multiple_of(i * step, step), step))
        return acc + jnp.sum(v.reshape(step // 8, 8, v.shape[-1]), axis=0)

    acc = lax.fori_loop(0, rows // step, body, jnp.zeros((8, FB), f32))
    return jnp.sum(acc, axis=0, keepdims=True)


def fold(v):
    return jnp.concatenate([v[:, : FB // 2], v[:, FB // 2:]], axis=0)


def unfold(v):
    return jnp.concatenate([v[0:4], v[4:8]], axis=1)


def total_of(vs):
    t = vs[0]
    for v in vs[1:]:
        t = t + v
    return t


def merge_moments(vs, n):
    vs = [unfold(v) for v in vs]
    t = total_of(vs)
    mean = t[0:2] * (1.0 / len(vs))
    m2 = t[2:4]
    for v in vs:
        d = v[0:2] - mean
        m2 = m2 + float(n) * d * d
    return jnp.concatenate([mean, m2], axis=0)


def kernel(
    a_ref, b_ref, ga_ref, gb_ref, loss_ref,
    na, nat, bn, braw, sb, ld1, sb2, ld2, ub, zbuf, gt, pbs, pbl, acc_a, acc_b,
    ex, lo, pay, vec, sbv, lacc, racc,
    ss, r1s, r2s, zs, g2s, g1s, bs, vs_, fs, ps, es, ls,
):
    bi = lax.axis_index("batch")
    fi = lax.axis_index("feat")
    y, zh, x = bi // 8, (bi // 4) % 2, bi % 4
    zl, core = fi // 2, fi % 2

    def dev(y_, zh_, x_, zl_, c_):
        return (((y_ + 4) % 4) * 8 + zh_ * 4 + ((x_ + 4) % 4), zl_ * 2 + c_)

    xdev = {d: dev(y, zh, x + d, zl, core) for d in (1, 2, 3)}
    ydev = {d: dev(y + d, zh, x, zl, core) for d in (1, 2, 3)}
    zhdev = dev(y, 1 - zh, x, zl, core)
    fdev = {1: dev(y, zh, x, zl, 1 - core), 2: dev(y, zh, x, 1 - zl, core),
            3: dev(y, zh, x, 1 - zl, 1 - core)}
    fidx = {0: fi, 1: zl * 2 + 1 - core, 2: (1 - zl) * 2 + core, 3: (1 - zl) * 2 + 1 - core}

    bar = pltpu.get_barrier_semaphore()
    partners = list(xdev.values()) + list(ydev.values()) + [zhdev] + list(fdev.values())
    for q in partners:
        pl.semaphore_signal(bar, inc=1, device_id=q, device_id_type=MESH)

    recv = {"r1": r1s, "r2": r2s, "z": zs, "g2": g2s, "g1": g1s, "b": bs, "v": vs_, "f": fs,
            "p": ps, "e": es, "l": ls}
    sent = {name: ss.at[i] for i, name in enumerate(recv)}

    def send(src, dst, key, to):
        cp = pltpu.make_async_remote_copy(
            src_ref=src, dst_ref=dst, send_sem=sent[key[0]], recv_sem=recv[key[0]].at[key[1:]],
            device_id=to, device_id_type=MESH)
        cp.start()

    def await_bytes(region, key):
        pltpu.make_async_remote_copy(
            src_ref=region, dst_ref=region, send_sem=sent[key[0]], recv_sem=recv[key[0]].at[key[1:]],
            device_id=zhdev, device_id_type=MESH).wait_recv()

    def await_sent(region, name):
        pltpu.make_async_remote_copy(
            src_ref=region, dst_ref=region, send_sem=sent[name], recv_sem=sent[name],
            device_id=zhdev, device_id_type=MESH).wait_send()

    mean_a = column_sum(lambda s: a_ref[s].astype(f32), ROWS) * (1.0 / ROWS)
    mean_b = column_sum(lambda s: b_ref[s].astype(f32), ROWS) * (1.0 / ROWS)

    def deviations(ref, mean):
        def f(s):
            d = ref[s].astype(f32) - mean
            return d * d
        return column_sum(f, ROWS)

    moments = jnp.concatenate(
        [mean_a, mean_b, deviations(a_ref, mean_a), deviations(b_ref, mean_b)], axis=0)
    pl.semaphore_wait(bar, len(partners))

    xto = [xdev[d] for d in (1, 2, 3)]
    yto = [ydev[d] for d in (1, 2, 3)]
    axes = {"x": (0, 4, x, xto), "y": (4, 4, y, yto), "z": (8, 2, zh, [zhdev])}

    def ex_send(e, axis, value):
        base, n, me, to = axes[axis]
        ex[e, base + me] = fold(value)
        for q in to:
            send(ex.at[e, base + me], ex.at[e, base + me], ("e", e, base // 4), q)

    def ex_wait(e, axis):
        base, n, me, to = axes[axis]
        await_bytes(ex.at[e, pl.ds(base, n - 1)], ("e", e, base // 4))
        return [ex[e, base + q] for q in range(n)]

    half = ROWS // 2

    def raw0():
        send(b_ref, braw.at[0], ("b", 0), fdev[1])
        send(b_ref.at[pl.ds(0, half)], braw.at[1, pl.ds(0, half)], ("b", 1), fdev[2])

    def raw1():
        send(b_ref.at[pl.ds(half, half)], braw.at[1, pl.ds(half, half)], ("b", 2), fdev[2])

    def fr():
        for i in (0, 1):
            s = pl.ds(i * half, half)
            await_bytes(braw.at[1, s], ("b", 1 + i))
            send(braw.at[1, s], braw.at[2, s], ("b", 3), fdev[1])

    ex_send(0, "z", moments)
    moments = merge_moments(ex_wait(0, "z"), ROWS)
    ex_send(0, "x", moments)
    moments = merge_moments(ex_wait(0, "x"), ROWS * 2)
    ex_send(0, "y", moments)
    moments = merge_moments(ex_wait(0, "y"), ROWS * 8)
    inv = 1.0 / jnp.sqrt(moments[2:4] * (1.0 / TOTAL) + eps_norm)
    vec[0] = fold(jnp.concatenate([moments[0:2], inv], axis=0))
    for k in (1, 2, 3):
        send(vec.at[0], vec.at[k], ("v", k - 1), fdev[k])

    def normalise(src, dst, mean, iv):
        def body(i, _):
            s = pl.ds(pl.multiple_of(i * 64, 64), 64)
            dst[s, :] = ((src[s, :].astype(f32) - mean) * iv).astype(bf16)
            return 0
        lax.fori_loop(0, ROWS // 64, body, 0)

    normalise(a_ref, na, moments[0:1], inv[0:1])
    normalise(b_ref, bn.at[0], moments[1:2], inv[1:2])
    for i in range(4):
        nat[pl.ds(i * 256, 256), :] = na[pl.ds(0, ROWS), pl.ds(i * 256, 256)].T

    def d0():
        s0 = column_sum(lambda s: na[s].astype(f32) * bn[0, s].astype(f32), ROWS)
        s1 = column_sum(lambda s: na[s].astype(f32), ROWS)
        s2 = column_sum(lambda s: bn[0, s].astype(f32), ROWS)
        ex_send(1, "x", jnp.concatenate([s0, s1, s2, jnp.zeros((1, FB), f32)], axis=0))
        lacc[...] = jnp.zeros_like(lacc)
        racc[...] = jnp.zeros_like(racc)
        pay[...] = jnp.zeros_like(pay)

    def d1():
        ex_send(1, "y", unfold(total_of(ex_wait(1, "x"))))

    def d2():
        ex_send(1, "z", unfold(total_of(ex_wait(1, "y"))))

    def d3():
        sbv[0] = total_of(ex_wait(1, "z")) * (1.0 / TOTAL)
        for k in (1, 2, 3):
            send(sbv.at[0], sbv.at[k], ("f", 0), fdev[k])

    def d4():
        await_bytes(sbv.at[pl.ds(1, 3)], ("f", 0))
        rows = lax.broadcasted_iota(jnp.int32, (16, FB), 0)

        def two_terms(v):
            hi = v.astype(bf16).astype(f32)
            return jnp.where(rows == 0, hi, jnp.where(rows == 1, v - hi, 0.0)).astype(bf16)

        na[pl.ds(ROWS, 16), :] = two_terms(unfold(sbv[0])[1:2])
        for k in range(4):
            bn[k, pl.ds(ROWS, 16), :] = two_terms(unfold(sbv[k])[2:3])

    p1 = (x, y)
    p2 = (y, x)
    nb1 = ((xdev[1], xdev[3]), (ydev[1], ydev[3]))
    nb2 = (nb1[1], nb1[0])

    def at(q, d):
        return (q + d) % 4

    def piece(base, q, size, lo_, n):
        return pl.ds(pl.multiple_of(base + q * size + lo_, 16), n)

    def ring_early(buf, land, base, q, size, nb, name, c, first):
        hf = size // 2
        right, left = nb
        if first:
            send(buf.at[piece(base, at(q, 2), size, 0, hf)], land(0), (name, c, 0), right)
            send(buf.at[piece(base, at(q, 2), size, hf, hf)], land(1), (name, c, 0), left)
        else:
            send(buf.at[piece(base, at(q, 1), size, hf, hf)], land(2), (name, c, 1), right)
            send(buf.at[piece(base, at(q, 3), size, 0, hf)], land(3), (name, c, 1), left)

    def ring_late(buf, land, base, q, size, nb, name, c):
        hf = size // 2
        for m, p in ((0, piece(base, at(q, 1), size, 0, hf)),
                     (1, piece(base, at(q, 3), size, hf, hf))):
            buf[p, :] = (buf[p, :].astype(f32) + land(m)[...].astype(f32)).astype(bf16)
            send(buf.at[p], land(4 + m), (name, c, 1), nb[m])

    def ring_fin(buf, land, base, q, size, out, obase):
        hf = size // 2
        for lo_, u, v in ((0, 3, 4), (hf, 2, 5)):
            out[pl.ds(obase + lo_, hf), :] = (
                buf[piece(base, q, size, lo_, hf), :].astype(f32)
                + land(u)[...].astype(f32) + land(v)[...].astype(f32)).astype(bf16)

    def gather_early(buf, base, q, size, nb, name, c):
        own = buf.at[piece(base, q, size, 0, size)]
        for to in nb:
            send(own, own, (name, c, 0), to)

    def gather_late(buf, base, q, size, nb, name, c):
        hf = size // 2
        ha = buf.at[piece(base, at(q, 3), size, 0, hf)]
        hb = buf.at[piece(base, at(q, 1), size, hf, hf)]
        send(ha, ha, (name, c, 1), nb[0])
        send(hb, hb, (name, c, 1), nb[1])

    H = (0, 1)

    def blk(c):
        return c // CPK

    def col(c):
        return (c % CPK) * W

    def land1(c, h):
        return lambda m: ld1.at[c, (m * 2 + h)]

    def land2(c, h):
        return lambda m: ld2.at[c, (m * 2 + h)]

    def dot(c):
        k = blk(c)
        if c % CPK == 0 and k > 0:
            if k == 1:
                await_bytes(braw.at[0], ("b", 0))
            if k == 3:
                await_bytes(braw.at[2], ("b", 3))
            await_bytes(vec.at[k], ("v", k - 1))
            v = unfold(vec[k])
            normalise(braw.at[k - 1], bn.at[k], v[1:2], v[3:4])
        n = 256

        def body(j, _):
            o = pl.multiple_of(j * n, n)
            i = pl.multiple_of(col(c) + j * n, n)
            sb[c, :, pl.ds(o, n)] = jnp.dot(
                nat[...], bn[k, pl.ds(0, ROWS), pl.ds(i, n)],
                preferred_element_type=f32).astype(bf16)
            return 0

        lax.fori_loop(0, W // n, body, 0)
        for first in (True, False):
            for h in H:
                ring_early(sb.at[c], land1(c, h), 512 * h, p1[h], 128, nb1[h], "r1", c, first)

    def la(c):
        await_bytes(ld1.at[c, pl.ds(0, 4)], ("r1", c, 0))
        for h in H:
            ring_late(sb.at[c], land1(c, h), 512 * h, p1[h], 128, nb1[h], "r1", c)

    def fa(c):
        await_bytes(ld1.at[c, pl.ds(4, 8)], ("r1", c, 1))
        for h in H:
            ring_fin(sb.at[c], land1(c, h), 512 * h, p1[h], 128, sb2.at[c, h], 0)
        for first in (True, False):
            for h in H:
                ring_early(sb2.at[c, h], land2(c, h), 0, p2[h], 32, nb2[h], "r2", c, first)

    def lb(c):
        await_bytes(ld2.at[c, pl.ds(0, 4)], ("r2", c, 0))
        for h in H:
            ring_late(sb2.at[c, h], land2(c, h), 0, p2[h], 32, nb2[h], "r2", c)

    def fb(c):
        await_bytes(ld2.at[c, pl.ds(4, 8)], ("r2", c, 1))
        for h in H:
            ring_fin(sb2.at[c, h], land2(c, h), 0, p2[h], 32, ub.at[c], 32 * h)
        send(ub.at[c], zbuf.at[c], ("z", c), zhdev)

    def base2(h):
        return 512 * h + 128 * p1[h] + 32 * p2[h]

    def ti(c):
        await_bytes(zbuf.at[c], ("z", c))
        k = blk(c)
        csum = jnp.zeros((8, W), f32)
        for h in H:
            base = base2(h)
            corr = (ub[c, pl.ds(32 * h, 32), :].astype(f32)
                    + zbuf[c, pl.ds(32 * h, 32), :].astype(f32)) * (1.0 / TOTAL)
            if k == 0:
                diag = jnp.broadcast_to(unfold(sbv[0])[0:1, col(c):col(c) + W], (32, W))
                rows = base + lax.broadcasted_iota(jnp.int32, (32, W), 0)
                cols = col(c) + lax.broadcasted_iota(jnp.int32, (32, W), 1)
                on = rows == cols
                gap = 1.0 - diag
                corr = jnp.where(on, diag, corr)
                ls_ = jnp.where(on, gap * gap, lam_off * corr * corr)
                g = jnp.where(on, -2.0 * gap, 2.0 * lam_off * corr)
            else:
                ls_ = lam_off * corr * corr
                g = 2.0 * lam_off * corr
            g = g.astype(bf16)
            gt[c, pl.ds(pl.multiple_of(base, 32), 32), :] = g
            prod = g.astype(f32) * corr
            lacc[...] += jnp.sum(ls_.reshape(4, 8, W), axis=0)
            csum = csum + jnp.sum(prod.reshape(4, 8, W), axis=0)
            racc[pl.ds(32 * h, 32), :] += total_of(
                [prod[:, t * 128:(t + 1) * 128] for t in range(W // 128)])
        for h in H:
            gather_early(gt.at[c], 512 * h + 128 * p1[h], p2[h], 32, nb2[h], "g2", c)
        pay[pl.ds(2 + k, 1), pl.ds(col(c), W)] = jnp.sum(csum, axis=0, keepdims=True)

    def f2(c):
        await_bytes(gt.at[c, pl.ds(0, 128)], ("g2", c, 0))
        for h in H:
            gather_late(gt.at[c], 512 * h + 128 * p1[h], p2[h], 32, nb2[h], "g2", c)

    def g1(c):
        await_bytes(gt.at[c, pl.ds(0, 64)], ("g2", c, 1))
        for h in H:
            gather_early(gt.at[c], 512 * h, p1[h], 128, nb1[h], "g1", c)

    def f1(c):
        await_bytes(gt.at[c, pl.ds(0, 512)], ("g1", c, 0))
        for h in H:
            gather_late(gt.at[c], 512 * h, p1[h], 128, nb1[h], "g1", c)

    started = []

    def bk(c):
        await_bytes(gt.at[c, pl.ds(0, 256)], ("g1", c, 1))
        k = blk(c)
        n = 256
        cs = pl.ds(col(c), W)
        j_ = c % CPK
        first = not started
        started.append(c)

        def body_b(j, _):
            o = pl.multiple_of(j * n, n)
            i = pl.multiple_of(col(c) + j * n, n)
            v = jnp.dot(na[...], gt[c, :, pl.ds(o, n)], preferred_element_type=f32)
            if k == 0:
                acc_b[:, pl.ds(i, n)] = v
            elif k == 2:
                pbs[1, :, pl.ds(i, n)] = (
                    v + pbl[2, :, pl.ds(i, n)].astype(f32)).astype(bf16)
            else:
                pbs[k - 1, :, pl.ds(i, n)] = v.astype(bf16)
            return 0

        if k == 2:
            await_bytes(pbl.at[2, :, cs], ("p", 2, j_))
        lax.fori_loop(0, W // n, body_b, 0)
        if k != 0:
            send(pbs.at[k - 1, :, cs], pbl.at[k - 1, :, cs], ("p", k - 1, j_),
                 fdev[2] if k == 2 else fdev[1])

        def body_a(j, _):
            o = pl.multiple_of(j * n, n)
            v = lax.dot_general(bn[k, :, cs], gt[c, pl.ds(o, n), :], (((1,), (1,)), ((), ())),
                                preferred_element_type=f32)
            if first:
                acc_a[:, pl.ds(o, n)] = v
            else:
                acc_a[:, pl.ds(o, n)] += v
            return 0

        lax.fori_loop(0, FB // n, body_a, 0)

    def lo_send(base, me, to, value):
        lo[base + me] = value
        for q in to:
            send(lo.at[base + me], lo.at[base + me], ("l", base // 4), q)

    def lo_wait(base):
        await_bytes(lo.at[pl.ds(base, 3)], ("l", base // 4))
        return total_of([lo[base + q] for q in range(4)])

    def e0():
        pay[0:1, 0:W] = jnp.sum(lacc[...], axis=0, keepdims=True)
        rs = jnp.sum(racc[...], axis=1, keepdims=True)
        lanes = lax.broadcasted_iota(jnp.int32, (32, FB), 1)
        rows = lax.broadcasted_iota(jnp.int32, (32, FB), 0)
        spa = jnp.zeros((1, FB), f32)
        for h in H:
            here = lanes == base2(h) + rows
            spa = spa + jnp.sum(jnp.where(here, rs[32 * h:32 * h + 32], 0.0), axis=0, keepdims=True)
        pay[1:2, :] = spa
        lo_send(0, x, xto, pay[...])

    def e1():
        lo_send(4, y, yto, lo_wait(0))

    def e2():
        lo_send(8, fi, [fdev[1], fdev[2], fdev[3]], lo_wait(4))

    def e3():
        t = lo_wait(8)
        loss_ref[...] = jnp.full((8, 128), jnp.sum(t[0:1]), f32)

    def end():
        mine = [lo[8 + fidx[k]] for k in range(4)]
        m_a = mine[0][1:2]
        m_b = total_of([mine[k][2 + k:3 + k] for k in range(4)])
        v = unfold(vec[0])
        inv_a, inv_b = v[2:3], v[3:4]
        c_a = acc_a[ROWS:ROWS + 1, :] + acc_a[ROWS + 1:ROWS + 2, :]

        def finish_a(i, _):
            s = pl.ds(pl.multiple_of(i * 32, 32), 32)
            ga_ref[s, :] = inv_a * (acc_a[s, :] - c_a - na[s, :].astype(f32) * m_a)
            return 0

        lax.fori_loop(0, ROWS // 32, finish_a, 0)
        for j in range(CPK):
            cs = pl.ds(j * W, W)
            await_bytes(pbl.at[0, :, cs], ("p", 0, j))
            await_bytes(pbl.at[1, :, cs], ("p", 1, j))

        def back_b(s):
            return acc_b[s, :] + pbl[0, s, :].astype(f32) + pbl[1, s, :].astype(f32)

        c_b = back_b(pl.ds(ROWS, 16))
        c_b = c_b[0:1] + c_b[1:2]

        def finish_b(i, _):
            s = pl.ds(pl.multiple_of(i * 32, 32), 32)
            gb_ref[s, :] = inv_b * (back_b(s) - c_b - bn[0, s, :].astype(f32) * m_b)
            return 0

        lax.fori_loop(0, ROWS // 32, finish_b, 0)

    order = [
        (raw0,), (d0,), (dot, 0), (raw1,), (dot, 1), (la, 0), (dot, 2), (d1,), (la, 1), (dot, 3),
        (fa, 0), (la, 2), (d2,), (fa, 1), (la, 3), (fa, 2), (lb, 1), (lb, 0), (fa, 3), (lb, 2),
        (fb, 1), (fr,), (dot, 4), (fb, 2), (lb, 3), (fb, 0), (d3,), (la, 4), (dot, 6), (fa, 4), (d4,),
        (fb, 3), (la, 6), (dot, 7), (lb, 4), (fa, 6), (dot, 5), (lb, 6), (la, 7), (fb, 4), (la, 5),
        (ti, 1), (ti, 2), (fb, 6), (ti, 4), (fa, 7), (fa, 5), (ti, 6), (f2, 4), (lb, 7), (ti, 0),
        (lb, 5), (f2, 6), (g1, 4), (fb, 7), (fb, 5), (g1, 6), (f2, 0), (ti, 7), (ti, 5), (f1, 6),
        (ti, 3), (f2, 2), (f2, 1), (f2, 7), (f2, 5), (f1, 4), (e0,), (bk, 6), (g1, 7), (g1, 5),
        (f2, 3), (bk, 4), (f1, 7), (e1,), (f1, 5), (g1, 3), (g1, 2), (g1, 1), (bk, 7), (f1, 3), (e2,),
        (bk, 5), (e3,), (f1, 2), (g1, 0), (f1, 1), (bk, 3), (bk, 2), (f1, 0), (bk, 1), (bk, 0), (end,),
    ]
    for step, *args in order:
        step(*args)

    for region, name in (
        (ld1, "r1"), (ld2, "r2"), (zbuf, "z"), (gt.at[:, pl.ds(0, 192)], "g2"),
        (gt.at[:, pl.ds(0, 768)], "g1"), (braw, "b"), (vec.at[pl.ds(1, 3)], "v"),
        (sbv.at[pl.ds(1, 3)], "f"), (pbl, "p"), (ex.at[:, pl.ds(0, 7)], "e"),
        (lo.at[pl.ds(0, 9)], "l"),
    ):
        await_sent(region, name)


def shards(view_a, view_b):
    vm = pl.BlockSpec(memory_space=pltpu.VMEM)
    dma = pltpu.SemaphoreType.DMA
    scratch = [
        pltpu.VMEM((RX, FB), bf16),
        pltpu.VMEM((FB, ROWS), bf16),
        pltpu.VMEM((4, RX, FB), bf16),
        pltpu.VMEM((3, ROWS, FB), bf16),
        pltpu.VMEM((NCH, FB, W), bf16),
        pltpu.VMEM((NCH, 12, 64, W), bf16),
        pltpu.VMEM((NCH, 2, 128, W), bf16),
        pltpu.VMEM((NCH, 12, 16, W), bf16),
        pltpu.VMEM((NCH, 64, W), bf16),
        pltpu.VMEM((NCH, 64, W), bf16),
        pltpu.VMEM((NCH, FB, W), bf16),
        pltpu.VMEM((3, RX, FB), bf16),
        pltpu.VMEM((3, RX, FB), bf16),
        pltpu.VMEM((RX, FB), f32),
        pltpu.VMEM((RX, FB), f32),
        pltpu.VMEM((2, 10, 8, FB // 2), f32),
        pltpu.VMEM((12, 8, FB), f32),
        pltpu.VMEM((8, FB), f32),
        pltpu.VMEM((4, 8, FB // 2), f32),
        pltpu.VMEM((4, 8, FB // 2), f32),
        pltpu.VMEM((8, W), f32),
        pltpu.VMEM((64, 128), f32),
        dma((11,)),
        dma((NCH, 2)), dma((NCH, 2)), dma((NCH,)), dma((NCH, 2)), dma((NCH, 2)),
        dma((4,)), dma((3,)), dma((1,)), dma((3, CPK)), dma((2, 3)), dma((3,)),
    ]
    ga, gb, loss = pl.pallas_call(
        kernel,
        out_shape=(
            jax.ShapeDtypeStruct((ROWS, FB), f32),
            jax.ShapeDtypeStruct((ROWS, FB), f32),
            jax.ShapeDtypeStruct((8, 128), f32),
        ),
        in_specs=[vm, vm],
        out_specs=(vm, vm, vm),
        scratch_shapes=scratch,
        compiler_params=pltpu.CompilerParams(
            collective_id=0, has_side_effects=True, vmem_limit_bytes=60 * 2**20),
        name="barlow",
    )(view_a, view_b)
    return ga, gb, loss[0, 0]


def solution(mesh):
    return jax.shard_map(
        shards,
        mesh=mesh,
        in_specs=(P("batch", "feat"), P("batch", "feat")),
        out_specs=(P("batch", "feat"), P("batch", "feat"), P()),
        check_vma=False,
    )
```

time: 870 us -> 134 us (0.15)
  blocking collectives: 436 us -> 0 us
  waiting for transfers between devices: 374 us -> 0 us
  Pallas kernels: 0 us -> 127 us
  matrix products: 31.1 us -> 0 us
  other arithmetic: 15 us -> 0 us
  between operations: 13.9 us -> 0.64 us
    psum x4 -> x0, blocking collectives: 436 us -> none  [the longest x1 183 us: shards(): lax.psum((jnp.sum(back_a, axis=0), jnp.sum(back_a * float_a, axis=0), jnp...]
    reduce_scatter x2 -> x0, waiting for transfers between devices: 228 us -> none  [the longest x1 225 us: shards(): lax.psum_scatter(lax.dot_general(columns, norm_a, (((0,), (0,)), ((), ())...]
    all_gather x2 -> x0, waiting for transfers between devices: 146 us -> none  [the longest x1 104 us: shards(): piece = lax.all_gather(grad_tile, 'batch', axis=0, tiled=True)]
    pallas_call x0 -> x1, Pallas kernels: none -> 127 us  [shards(): pl.pallas_call(kernel, out_shape=(jax.ShapeDtypeStruct((ROWS, FB), f32),...]
    dot_general x3 -> x0, matrix products: 31.1 us -> none  [the longest x1 10.6 us: shards(): back_a = jnp.dot(columns, piece, preferred_element_type=jnp.float32)]
  transfers between devices with their start and end apart: 4 -> 0, of which waited for: 4 -> 0; matrix products, arithmetic and copies ran while one was open for 1% -> 0% of each run, Pallas kernels for 0% -> 0%
where the time goes in v2:
time: 134 us; the launch traced here: 133 us
  Pallas kernels  127 us (95%)
  local copies, waits for them, and re-layouts  5.82 us (4%)
    pallas_call x1, Pallas kernels, shards(): pl.pallas_call(kernel, out_shape=(jax.ShapeDtypeStruct((ROWS, FB), f32),...  127 us
    unnamed x4, local copies, waits for them, and re-layouts  4.63 us

profile of v2, /device:TPU:0, one launch (start us, length us, event | category | flops | bytes accessed | tf_op | source)
XLA Modules:
  0.0 133.5 jit_solution(17900628279209367575)
XLA Ops:
  0.6 127.0 %barlow.1 = (f32[512,1024]{1,0:T(8,128)}, f32[512,1024]{1,0:T(8,128)}, f32[8,128]{1,0:T(8,128)}) custom-call(bf16[512,1024]{1,0:T(8,128)(2,1)} %a_ref.1, bf16[512,1024]{1,0:T(8,128)(2,1)} %b_ref.1), custom_call_target="tpu_custom_call" | custom-call | tf_op jit(solution)/shard_map/barlow/pallas_call | solution.py:520
  127.7 1.2 slice.3
  128.9 0.0 copy-start
  128.9 3.3 %copy.7 = f32[512,1024]{1,0:T(8,128)} copy(f32[512,1024]{1,0:T(8,128)} %get-tuple-element.12) | data formatting | bytes 4194304
  132.2 0.0 copy-done
  132.2 1.3 copy.8
Async XLA Ops:
  128.9 3.3 %copy-start = (f32[512,1024]{1,0:T(8,128)S(1)}, f32[512,1024]{1,0:T(8,128)}, u32[]{:S(2)}) copy-start(f32[512,1024]{1,0:T(8,128)} %get-tuple-element.13) | copy-start | bytes 6291460

commit v3 on v2

--- a/solution.py
+++ b/solution.py
@@ -30,11 +30,13 @@
 
 
 def fold(v):
-    return jnp.concatenate([v[:, : FB // 2], v[:, FB // 2:]], axis=0)
+    w = v.shape[0] * FB // 8
+    return jnp.concatenate([v[:, p * w:(p + 1) * w] for p in range(FB // w)], axis=0)
 
 
 def unfold(v):
-    return jnp.concatenate([v[0:4], v[4:8]], axis=1)
+    r = v.shape[1] * 8 // FB
+    return jnp.concatenate([v[p * r:(p + 1) * r] for p in range(8 // r)], axis=1)
 
 
 def total_of(vs):
@@ -44,22 +46,11 @@
     return t
 
 
-def merge_moments(vs, n):
-    vs = [unfold(v) for v in vs]
-    t = total_of(vs)
-    mean = t[0:2] * (1.0 / len(vs))
-    m2 = t[2:4]
-    for v in vs:
-        d = v[0:2] - mean
-        m2 = m2 + float(n) * d * d
-    return jnp.concatenate([mean, m2], axis=0)
-
-
 def kernel(
     a_ref, b_ref, ga_ref, gb_ref, loss_ref,
     na, nat, bn, braw, sb, ld1, sb2, ld2, ub, zbuf, gt, pbs, pbl, acc_a, acc_b,
-    ex, lo, pay, vec, sbv, lacc, racc,
-    ss, r1s, r2s, zs, g2s, g1s, bs, vs_, fs, ps, es, ls,
+    ex, ex2, mg, mb, mrow, lo, pay, vec, db, dat, dg, sbv, lacc, racc,
+    ss, r1s, r2s, zs, g2s, g1s, bs, vs_, ws, fs, ps, es, e2s, ms, mbs, ls,
 ):
     bi = lax.axis_index("batch")
     fi = lax.axis_index("feat")
@@ -81,8 +72,8 @@
     for q in partners:
         pl.semaphore_signal(bar, inc=1, device_id=q, device_id_type=MESH)
 
-    recv = {"r1": r1s, "r2": r2s, "z": zs, "g2": g2s, "g1": g1s, "b": bs, "v": vs_, "f": fs,
-            "p": ps, "e": es, "l": ls}
+    recv = {"r1": r1s, "r2": r2s, "z": zs, "g2": g2s, "g1": g1s, "b": bs, "v": vs_, "w": ws,
+            "f": fs, "p": ps, "e": es, "d": e2s, "m": ms, "n": mbs, "l": ls}
     sent = {name: ss.at[i] for i, name in enumerate(recv)}
 
     def send(src, dst, key, to):
@@ -104,34 +95,33 @@
     mean_a = column_sum(lambda s: a_ref[s].astype(f32), ROWS) * (1.0 / ROWS)
     mean_b = column_sum(lambda s: b_ref[s].astype(f32), ROWS) * (1.0 / ROWS)
 
-    def deviations(ref, mean):
-        def f(s):
-            d = ref[s].astype(f32) - mean
-            return d * d
-        return column_sum(f, ROWS)
-
-    moments = jnp.concatenate(
-        [mean_a, mean_b, deviations(a_ref, mean_a), deviations(b_ref, mean_b)], axis=0)
+    mrow[0] = jnp.broadcast_to(mean_b, (8, FB))
+    mb[0] = fold(mean_b)
+    for i in range(4):
+        s = slice(i * 256, (i + 1) * 256)
+        nat[s, :] = (a_ref[:, s].astype(f32) - mean_a[:, s]).astype(bf16).T
     pl.semaphore_wait(bar, len(partners))
 
     xto = [xdev[d] for d in (1, 2, 3)]
     yto = [ydev[d] for d in (1, 2, 3)]
     axes = {"x": (0, 4, x, xto), "y": (4, 4, y, yto), "z": (8, 2, zh, [zhdev])}
 
-    def ex_send(e, axis, value):
+    def ex_send(buf, name, axis, value):
         base, n, me, to = axes[axis]
-        ex[e, base + me] = fold(value)
+        buf[base + me] = value
         for q in to:
-            send(ex.at[e, base + me], ex.at[e, base + me], ("e", e, base // 4), q)
-
-    def ex_wait(e, axis):
+            send(buf.at[base + me], buf.at[base + me], (name, base // 4), q)
+
+    def ex_wait(buf, name, axis):
         base, n, me, to = axes[axis]
-        await_bytes(ex.at[e, pl.ds(base, n - 1)], ("e", e, base // 4))
-        return [ex[e, base + q] for q in range(n)]
+        await_bytes(buf.at[pl.ds(base, n - 1)], (name, base // 4))
+        return total_of([buf[base + q] for q in range(n)])
 
     half = ROWS // 2
 
     def raw0():
+        for k in (1, 2, 3):
+            send(mb.at[0], mb.at[k], ("n", k - 1), fdev[k])
         send(b_ref, braw.at[0], ("b", 0), fdev[1])
         send(b_ref.at[pl.ds(0, half)], braw.at[1, pl.ds(0, half)], ("b", 1), fdev[2])
 
@@ -144,16 +134,65 @@
             await_bytes(braw.at[1, s], ("b", 1 + i))
             send(braw.at[1, s], braw.at[2, s], ("b", 3), fdev[1])
 
-    ex_send(0, "z", moments)
-    moments = merge_moments(ex_wait(0, "z"), ROWS)
-    ex_send(0, "x", moments)
-    moments = merge_moments(ex_wait(0, "x"), ROWS * 2)
-    ex_send(0, "y", moments)
-    moments = merge_moments(ex_wait(0, "y"), ROWS * 8)
-    inv = 1.0 / jnp.sqrt(moments[2:4] * (1.0 / TOTAL) + eps_norm)
-    vec[0] = fold(jnp.concatenate([moments[0:2], inv], axis=0))
-    for k in (1, 2, 3):
-        send(vec.at[0], vec.at[k], ("v", k - 1), fdev[k])
+    def group(n):
+        return {1: (zh * 4 + y) * 4 + x, 4: (zh * 4 + y) * 4, 16: zh * 16}[n]
+
+    def mg_send(n, axis):
+        r = pl.ds(pl.multiple_of(group(n) * 16, 16), n * 16)
+        for q in axes[axis][3]:
+            send(mg.at[r], mg.at[r], ("m", axes[axis][0] // 4), q)
+
+    def s0():
+        def sums(i, acc):
+            s = pl.ds(pl.multiple_of(i * 32, 32), 32)
+            u = a_ref[s].astype(f32) - mean_a
+            v = b_ref[s].astype(f32) - mean_b
+            return tuple(t + jnp.sum(p.reshape(4, 8, FB), axis=0)
+                         for t, p in zip(acc, (u * u, v * v, u * v)))
+
+        z8 = jnp.zeros((8, FB), f32)
+        acc = lax.fori_loop(0, ROWS // 32, sums, (z8, z8, z8))
+        mg[pl.ds(pl.multiple_of(group(1) * 16, 16), 16), :] = jnp.concatenate(
+            [m[:, p * 128:(p + 1) * 128] for p in range(8) for m in (mean_a, mean_b)], axis=0)
+        mg_send(1, "x")
+        ex_send(ex, "e", "x", fold(jnp.concatenate(
+            [jnp.sum(t, axis=0, keepdims=True) for t in acc] + [jnp.zeros((1, FB), f32)], axis=0)))
+
+    def s1():
+        await_bytes(mg.at[pl.ds(0, 48)], ("m", 0))
+        mg_send(4, "y")
+        ex_send(ex, "e", "y", ex_wait(ex, "e", "x"))
+
+    def s2():
+        await_bytes(mg.at[pl.ds(0, 192)], ("m", 1))
+        mg_send(16, "z")
+        ex_send(ex, "e", "z", ex_wait(ex, "e", "y"))
+
+    def s3():
+        await_bytes(mg.at[pl.ds(0, 256)], ("m", 2))
+        t = unfold(ex_wait(ex, "e", "z"))
+        db[:, 32:128, :] = jnp.zeros((4, 96, FB), bf16)
+        stat = []
+        for p in range(8):
+            s = slice(p * 128, (p + 1) * 128)
+            da = mg[pl.ds(2 * p, 32, stride=16), :]
+            dbb = mg[pl.ds(2 * p + 1, 32, stride=16), :]
+            mu_a = jnp.sum(da, axis=0, keepdims=True) * (1.0 / 32)
+            mu_b = jnp.sum(dbb, axis=0, keepdims=True) * (1.0 / 32)
+            da = da - mu_a
+            dbb = dbb - mu_b
+            sq = [jnp.sum(u * v, axis=0, keepdims=True) * float(ROWS) + t[i:i + 1, s]
+                  for i, (u, v) in enumerate(((da, da), (dbb, dbb), (da, dbb)))]
+            inv_a = 1.0 / jnp.sqrt(sq[0] * (1.0 / TOTAL) + eps_norm)
+            inv_b = 1.0 / jnp.sqrt(sq[1] * (1.0 / TOTAL) + eps_norm)
+            stat.append(jnp.concatenate([mu_a, mu_b, inv_a, inv_b], axis=0))
+            dg[:, s] = jnp.broadcast_to(sq[2] * (1.0 / TOTAL) * inv_a * inv_b, (8, 128))
+            db[0, 0:32, s] = dbb.astype(bf16)
+            dat[s, :] = jnp.concatenate([da, inv_a, jnp.zeros((95, 128), f32)], axis=0).T
+        vec[0] = fold(jnp.concatenate(stat, axis=1))
+        for k in (1, 2, 3):
+            send(vec.at[0], vec.at[k], ("v", k - 1), fdev[k])
+            send(db.at[0, pl.ds(0, 32)], db.at[k, pl.ds(0, 32)], ("w", k - 1), fdev[k])
 
     def normalise(src, dst, mean, iv):
         def body(i, _):
@@ -162,28 +201,28 @@
             return 0
         lax.fori_loop(0, ROWS // 64, body, 0)
 
-    normalise(a_ref, na, moments[0:1], inv[0:1])
-    normalise(b_ref, bn.at[0], moments[1:2], inv[1:2])
-    for i in range(4):
-        nat[pl.ds(i * 256, 256), :] = na[pl.ds(0, ROWS), pl.ds(i * 256, 256)].T
+    def nm(k):
+        if k > 0:
+            await_bytes(vec.at[k], ("v", k - 1))
+            await_bytes(db.at[k, pl.ds(0, 32)], ("w", k - 1))
+        v = unfold(vec[k])
+        normalise(braw.at[k - 1] if k else b_ref, bn.at[k], v[1:2], v[3:4])
+        if k == 0:
+            normalise(a_ref, na, v[0:1], v[2:3])
 
     def d0():
-        s0 = column_sum(lambda s: na[s].astype(f32) * bn[0, s].astype(f32), ROWS)
-        s1 = column_sum(lambda s: na[s].astype(f32), ROWS)
-        s2 = column_sum(lambda s: bn[0, s].astype(f32), ROWS)
-        ex_send(1, "x", jnp.concatenate([s0, s1, s2, jnp.zeros((1, FB), f32)], axis=0))
-        lacc[...] = jnp.zeros_like(lacc)
-        racc[...] = jnp.zeros_like(racc)
-        pay[...] = jnp.zeros_like(pay)
+        s1_ = column_sum(lambda s: na[s].astype(f32), ROWS)
+        s2_ = column_sum(lambda s: bn[0, s].astype(f32), ROWS)
+        ex_send(ex2, "d", "x", fold(jnp.concatenate([s1_, s2_], axis=0)))
 
     def d1():
-        ex_send(1, "y", unfold(total_of(ex_wait(1, "x"))))
+        ex_send(ex2, "d", "y", ex_wait(ex2, "d", "x"))
 
     def d2():
-        ex_send(1, "z", unfold(total_of(ex_wait(1, "y"))))
+        ex_send(ex2, "d", "z", ex_wait(ex2, "d", "y"))
 
     def d3():
-        sbv[0] = total_of(ex_wait(1, "z")) * (1.0 / TOTAL)
+        sbv[0] = ex_wait(ex2, "d", "z") * (1.0 / TOTAL)
         for k in (1, 2, 3):
             send(sbv.at[0], sbv.at[k], ("f", 0), fdev[k])
 
@@ -195,9 +234,9 @@
             hi = v.astype(bf16).astype(f32)
             return jnp.where(rows == 0, hi, jnp.where(rows == 1, v - hi, 0.0)).astype(bf16)
 
-        na[pl.ds(ROWS, 16), :] = two_terms(unfold(sbv[0])[1:2])
+        na[pl.ds(ROWS, 16), :] = two_terms(unfold(sbv[0])[0:1])
         for k in range(4):
-            bn[k, pl.ds(ROWS, 16), :] = two_terms(unfold(sbv[k])[2:3])
+            bn[k, pl.ds(ROWS, 16), :] = two_terms(unfold(sbv[k])[1:2])
 
     p1 = (x, y)
     p2 = (y, x)
@@ -262,22 +301,22 @@
 
     def dot(c):
         k = blk(c)
+        src = b_ref if k == 0 else braw.at[k - 1]
         if c % CPK == 0 and k > 0:
             if k == 1:
                 await_bytes(braw.at[0], ("b", 0))
             if k == 3:
                 await_bytes(braw.at[2], ("b", 3))
-            await_bytes(vec.at[k], ("v", k - 1))
-            v = unfold(vec[k])
-            normalise(braw.at[k - 1], bn.at[k], v[1:2], v[3:4])
+            await_bytes(mb.at[k], ("n", k - 1))
+            mrow[k] = jnp.broadcast_to(unfold(mb[k]), (8, FB))
         n = 256
 
         def body(j, _):
             o = pl.multiple_of(j * n, n)
             i = pl.multiple_of(col(c) + j * n, n)
+            centered = (src[:, pl.ds(i, n)].astype(f32) - mrow[k, 0:1, pl.ds(i, n)]).astype(bf16)
             sb[c, :, pl.ds(o, n)] = jnp.dot(
-                nat[...], bn[k, pl.ds(0, ROWS), pl.ds(i, n)],
-                preferred_element_type=f32).astype(bf16)
+                nat[...], centered, preferred_element_type=f32).astype(bf16)
             return 0
 
         lax.fori_loop(0, W // n, body, 0)
@@ -316,12 +355,17 @@
         await_bytes(zbuf.at[c], ("z", c))
         k = blk(c)
         csum = jnp.zeros((8, W), f32)
+        inv_b = unfold(vec[k])[3:4, col(c):col(c) + W]
         for h in H:
             base = base2(h)
+            mine = dat[pl.ds(pl.multiple_of(base, 32), 32), :]
             corr = (ub[c, pl.ds(32 * h, 32), :].astype(f32)
-                    + zbuf[c, pl.ds(32 * h, 32), :].astype(f32)) * (1.0 / TOTAL)
+                    + zbuf[c, pl.ds(32 * h, 32), :].astype(f32)
+                    + float(ROWS) * jnp.dot(mine.astype(bf16), db[k, :, col(c):col(c) + W],
+                                            preferred_element_type=f32))
+            corr = corr * (mine[:, 32:33] * (1.0 / TOTAL)) * inv_b
             if k == 0:
-                diag = jnp.broadcast_to(unfold(sbv[0])[0:1, col(c):col(c) + W], (32, W))
+                diag = jnp.broadcast_to(dg[0:1, col(c):col(c) + W], (32, W))
                 rows = base + lax.broadcasted_iota(jnp.int32, (32, W), 0)
                 cols = col(c) + lax.broadcasted_iota(jnp.int32, (32, W), 1)
                 on = rows == cols
@@ -464,24 +508,31 @@
 
         lax.fori_loop(0, ROWS // 32, finish_b, 0)
 
+    lacc[...] = jnp.zeros_like(lacc)
+    racc[...] = jnp.zeros_like(racc)
+    pay[...] = jnp.zeros_like(pay)
+
     order = [
-        (raw0,), (d0,), (dot, 0), (raw1,), (dot, 1), (la, 0), (dot, 2), (d1,), (la, 1), (dot, 3),
-        (fa, 0), (la, 2), (d2,), (fa, 1), (la, 3), (fa, 2), (lb, 1), (lb, 0), (fa, 3), (lb, 2),
-        (fb, 1), (fr,), (dot, 4), (fb, 2), (lb, 3), (fb, 0), (d3,), (la, 4), (dot, 6), (fa, 4), (d4,),
-        (fb, 3), (la, 6), (dot, 7), (lb, 4), (fa, 6), (dot, 5), (lb, 6), (la, 7), (fb, 4), (la, 5),
-        (ti, 1), (ti, 2), (fb, 6), (ti, 4), (fa, 7), (fa, 5), (ti, 6), (f2, 4), (lb, 7), (ti, 0),
-        (lb, 5), (f2, 6), (g1, 4), (fb, 7), (fb, 5), (g1, 6), (f2, 0), (ti, 7), (ti, 5), (f1, 6),
-        (ti, 3), (f2, 2), (f2, 1), (f2, 7), (f2, 5), (f1, 4), (e0,), (bk, 6), (g1, 7), (g1, 5),
-        (f2, 3), (bk, 4), (f1, 7), (e1,), (f1, 5), (g1, 3), (g1, 2), (g1, 1), (bk, 7), (f1, 3), (e2,),
-        (bk, 5), (e3,), (f1, 2), (g1, 0), (f1, 1), (bk, 3), (bk, 2), (f1, 0), (bk, 1), (bk, 0), (end,),
+        (raw0,), (raw1,), (dot, 0), (s0,), (dot, 1), (dot, 2), (s1,), (la, 0), (dot, 3), (la, 1),
+        (la, 2), (fa, 0), (s2,), (la, 3), (fa, 2), (lb, 0), (fa, 1), (fa, 3), (lb, 2), (fr,), (dot, 4),
+        (fb, 0), (lb, 1), (lb, 3), (fb, 2), (la, 4), (dot, 6), (s3,), (fa, 4), (la, 6), (dot, 5),
+        (fb, 1), (lb, 4), (nm, 1), (fb, 3), (fa, 6), (dot, 7), (nm, 0), (fb, 4), (lb, 6), (la, 5),
+        (d0,), (nm, 3), (la, 7), (ti, 3), (fb, 6), (nm, 2), (ti, 4), (fa, 5), (ti, 0), (d1,), (fa, 7),
+        (ti, 6), (lb, 5), (f2, 4), (ti, 1), (ti, 2), (d2,), (lb, 7), (f2, 6), (g1, 4), (fb, 5),
+        (fb, 7), (g1, 6), (f2, 2), (d3,), (ti, 5), (f2, 0), (ti, 7), (d4,), (f1, 6), (e0,), (f1, 4),
+        (f2, 7), (f2, 5), (g1, 0), (bk, 6), (e1,), (g1, 7), (g1, 5), (bk, 4), (e2,), (f1, 7), (f2, 1),
+        (f2, 3), (g1, 2), (f1, 5), (f1, 0), (bk, 7), (g1, 3), (g1, 1), (f1, 2), (bk, 5), (f1, 3),
+        (e3,), (bk, 0), (f1, 1), (bk, 2), (bk, 3), (bk, 1), (end,),
     ]
     for step, *args in order:
         step(*args)
 
     for region, name in (
+        (mg.at[pl.ds(0, 48 + 192 + 256)], "m"), (mb.at[pl.ds(1, 3)], "n"),
+        (db.at[pl.ds(1, 3), pl.ds(0, 32)], "w"), (ex2.at[pl.ds(0, 7)], "d"),
         (ld1, "r1"), (ld2, "r2"), (zbuf, "z"), (gt.at[:, pl.ds(0, 192)], "g2"),
         (gt.at[:, pl.ds(0, 768)], "g1"), (braw, "b"), (vec.at[pl.ds(1, 3)], "v"),
-        (sbv.at[pl.ds(1, 3)], "f"), (pbl, "p"), (ex.at[:, pl.ds(0, 7)], "e"),
+        (sbv.at[pl.ds(1, 3)], "f"), (pbl, "p"), (ex.at[pl.ds(0, 7)], "e"),
         (lo.at[pl.ds(0, 9)], "l"),
     ):
         await_sent(region, name)
@@ -506,16 +557,24 @@
         pltpu.VMEM((3, RX, FB), bf16),
         pltpu.VMEM((RX, FB), f32),
         pltpu.VMEM((RX, FB), f32),
-        pltpu.VMEM((2, 10, 8, FB // 2), f32),
+        pltpu.VMEM((10, 8, FB // 2), f32),
+        pltpu.VMEM((10, 8, FB // 4), f32),
+        pltpu.VMEM((32 * 16, 128), f32),
+        pltpu.VMEM((4, 8, FB // 8), f32),
+        pltpu.VMEM((4, 8, FB), f32),
         pltpu.VMEM((12, 8, FB), f32),
         pltpu.VMEM((8, FB), f32),
         pltpu.VMEM((4, 8, FB // 2), f32),
-        pltpu.VMEM((4, 8, FB // 2), f32),
+        pltpu.VMEM((4, 128, FB), bf16),
+        pltpu.VMEM((FB, 128), f32),
+        pltpu.VMEM((8, FB), f32),
+        pltpu.VMEM((4, 8, FB // 4), f32),
         pltpu.VMEM((8, W), f32),
         pltpu.VMEM((64, 128), f32),
-        dma((11,)),
+        dma((15,)),
         dma((NCH, 2)), dma((NCH, 2)), dma((NCH,)), dma((NCH, 2)), dma((NCH, 2)),
-        dma((4,)), dma((3,)), dma((1,)), dma((3, CPK)), dma((2, 3)), dma((3,)),
+        dma((4,)), dma((3,)), dma((3,)), dma((1,)), dma((3, CPK)), dma((3,)), dma((3,)), dma((3,)),
+        dma((3,)), dma((3,)),
     ]
     ga, gb, loss = pl.pallas_call(
         kernel,

time: 134 us -> 121 us (0.903)
  Pallas kernels: 127 us -> 115 us
    pallas_call x1, Pallas kernels: 127 us -> 115 us  [shards(): pl.pallas_call(kernel, out_shape=(jax.ShapeDtypeStruct((ROWS, FB), f32),...]
where the time goes in v3:
time: 121 us
  Pallas kernels  115 us (95%)
  local copies, waits for them, and re-layouts  5.82 us (5%)
    pallas_call x1, Pallas kernels, shards(): pl.pallas_call(kernel, out_shape=(jax.ShapeDtypeStruct((ROWS, FB), f32),...  115 us
    unnamed x4, local copies, waits for them, and re-layouts  4.63 us

profile of v3, /device:TPU:0, one launch (start us, length us, event | category | flops | bytes accessed | tf_op | source)
XLA Modules:
  0.0 121.0 jit_solution(8614683923231104351)
XLA Ops:
  0.6 114.6 %barlow.1 = (f32[512,1024]{1,0:T(8,128)}, f32[512,1024]{1,0:T(8,128)}, f32[8,128]{1,0:T(8,128)}) custom-call(bf16[512,1024]{1,0:T(8,128)(2,1)} %a_ref.1, bf16[512,1024]{1,0:T(8,128)(2,1)} %b_ref.1), custom_call_target="tpu_custom_call" | custom-call | tf_op jit(solution)/shard_map/barlow/pallas_call | solution.py:579
  115.2 1.2 slice.3
  116.4 0.0 copy-start
  116.4 3.3 %copy.7 = f32[512,1024]{1,0:T(8,128)} copy(f32[512,1024]{1,0:T(8,128)} %get-tuple-element.12) | data formatting | bytes 4194304
  119.7 0.0 copy-done
  119.7 1.3 %copy.8 = f32[512,1024]{1,0:T(8,128)} copy(f32[512,1024]{1,0:T(8,128)S(1)} %copy-done) | data formatting | bytes 4194304
Async XLA Ops:
  116.4 3.3 %copy-start = (f32[512,1024]{1,0:T(8,128)S(1)}, f32[512,1024]{1,0:T(8,128)}, u32[]{:S(2)}) copy-start(f32[512,1024]{1,0:T(8,128)} %get-tuple-element.13) | copy-start | bytes 6291460

commit v4 on v3

--- a/solution.py
+++ b/solution.py
@@ -92,6 +92,12 @@
             src_ref=region, dst_ref=region, send_sem=sent[name], recv_sem=sent[name],
             device_id=zhdev, device_id_type=MESH).wait_send()
 
+    def multiply(c, src):
+        k = c // CPK
+        o = c % CPK * W
+        centered = (src[:, o:o + W].astype(f32) - mrow[k, 0:1, o:o + W]).astype(bf16)
+        sb[c] = jnp.dot(nat[...], centered, preferred_element_type=f32).astype(bf16)
+
     mean_a = column_sum(lambda s: a_ref[s].astype(f32), ROWS) * (1.0 / ROWS)
     mean_b = column_sum(lambda s: b_ref[s].astype(f32), ROWS) * (1.0 / ROWS)
 
@@ -100,6 +106,21 @@
     for i in range(4):
         s = slice(i * 256, (i + 1) * 256)
         nat[s, :] = (a_ref[:, s].astype(f32) - mean_a[:, s]).astype(bf16).T
+    multiply(0, b_ref)
+
+    def local_sums(i, acc):
+        s = pl.ds(pl.multiple_of(i * 32, 32), 32)
+        u = a_ref[s].astype(f32) - mean_a
+        v = b_ref[s].astype(f32) - mean_b
+        return tuple(t + jnp.sum(p.reshape(4, 8, FB), axis=0)
+                     for t, p in zip(acc, (u * u, v * v, u * v)))
+
+    z8 = jnp.zeros((8, FB), f32)
+    local = [jnp.sum(t, axis=0, keepdims=True)
+             for t in lax.fori_loop(0, ROWS // 32, local_sums, (z8, z8, z8))]
+    lacc[...] = jnp.zeros_like(lacc)
+    racc[...] = jnp.zeros_like(racc)
+    pay[...] = jnp.zeros_like(pay)
     pl.semaphore_wait(bar, len(partners))
 
     xto = [xdev[d] for d in (1, 2, 3)]
@@ -143,20 +164,11 @@
             send(mg.at[r], mg.at[r], ("m", axes[axis][0] // 4), q)
 
     def s0():
-        def sums(i, acc):
-            s = pl.ds(pl.multiple_of(i * 32, 32), 32)
-            u = a_ref[s].astype(f32) - mean_a
-            v = b_ref[s].astype(f32) - mean_b
-            return tuple(t + jnp.sum(p.reshape(4, 8, FB), axis=0)
-                         for t, p in zip(acc, (u * u, v * v, u * v)))
-
-        z8 = jnp.zeros((8, FB), f32)
-        acc = lax.fori_loop(0, ROWS // 32, sums, (z8, z8, z8))
         mg[pl.ds(pl.multiple_of(group(1) * 16, 16), 16), :] = jnp.concatenate(
             [m[:, p * 128:(p + 1) * 128] for p in range(8) for m in (mean_a, mean_b)], axis=0)
         mg_send(1, "x")
         ex_send(ex, "e", "x", fold(jnp.concatenate(
-            [jnp.sum(t, axis=0, keepdims=True) for t in acc] + [jnp.zeros((1, FB), f32)], axis=0)))
+            local + [jnp.zeros((1, FB), f32)], axis=0)))
 
     def s1():
         await_bytes(mg.at[pl.ds(0, 48)], ("m", 0))
@@ -309,17 +321,8 @@
                 await_bytes(braw.at[2], ("b", 3))
             await_bytes(mb.at[k], ("n", k - 1))
             mrow[k] = jnp.broadcast_to(unfold(mb[k]), (8, FB))
-        n = 256
-
-        def body(j, _):
-            o = pl.multiple_of(j * n, n)
-            i = pl.multiple_of(col(c) + j * n, n)
-            centered = (src[:, pl.ds(i, n)].astype(f32) - mrow[k, 0:1, pl.ds(i, n)]).astype(bf16)
-            sb[c, :, pl.ds(o, n)] = jnp.dot(
-                nat[...], centered, preferred_element_type=f32).astype(bf16)
-            return 0
-
-        lax.fori_loop(0, W // n, body, 0)
+        if c > 0:
+            multiply(c, src)
         for first in (True, False):
             for h in H:
                 ring_early(sb.at[c], land1(c, h), 512 * h, p1[h], 128, nb1[h], "r1", c, first)
@@ -407,43 +410,28 @@
     def bk(c):
         await_bytes(gt.at[c, pl.ds(0, 256)], ("g1", c, 1))
         k = blk(c)
-        n = 256
         cs = pl.ds(col(c), W)
         j_ = c % CPK
         first = not started
         started.append(c)
 
-        def body_b(j, _):
-            o = pl.multiple_of(j * n, n)
-            i = pl.multiple_of(col(c) + j * n, n)
-            v = jnp.dot(na[...], gt[c, :, pl.ds(o, n)], preferred_element_type=f32)
-            if k == 0:
-                acc_b[:, pl.ds(i, n)] = v
-            elif k == 2:
-                pbs[1, :, pl.ds(i, n)] = (
-                    v + pbl[2, :, pl.ds(i, n)].astype(f32)).astype(bf16)
-            else:
-                pbs[k - 1, :, pl.ds(i, n)] = v.astype(bf16)
-            return 0
-
         if k == 2:
             await_bytes(pbl.at[2, :, cs], ("p", 2, j_))
-        lax.fori_loop(0, W // n, body_b, 0)
-        if k != 0:
+        v = jnp.dot(na[...], gt[c], preferred_element_type=f32)
+        if k == 0:
+            acc_b[:, cs] = v
+        else:
+            if k == 2:
+                v = v + pbl[2, :, cs].astype(f32)
+            pbs[k - 1, :, cs] = v.astype(bf16)
             send(pbs.at[k - 1, :, cs], pbl.at[k - 1, :, cs], ("p", k - 1, j_),
                  fdev[2] if k == 2 else fdev[1])
-
-        def body_a(j, _):
-            o = pl.multiple_of(j * n, n)
-            v = lax.dot_general(bn[k, :, cs], gt[c, pl.ds(o, n), :], (((1,), (1,)), ((), ())),
-                                preferred_element_type=f32)
-            if first:
-                acc_a[:, pl.ds(o, n)] = v
-            else:
-                acc_a[:, pl.ds(o, n)] += v
-            return 0
-
-        lax.fori_loop(0, FB // n, body_a, 0)
+        u = lax.dot_general(bn[k, :, cs], gt[c], (((1,), (1,)), ((), ())),
+                            preferred_element_type=f32)
+        if first:
+            acc_a[...] = u
+        else:
+            acc_a[...] += u
 
     def lo_send(base, me, to, value):
         lo[base + me] = value
@@ -508,21 +496,17 @@
 
         lax.fori_loop(0, ROWS // 32, finish_b, 0)
 
-    lacc[...] = jnp.zeros_like(lacc)
-    racc[...] = jnp.zeros_like(racc)
-    pay[...] = jnp.zeros_like(pay)
-
     order = [
-        (raw0,), (raw1,), (dot, 0), (s0,), (dot, 1), (dot, 2), (s1,), (la, 0), (dot, 3), (la, 1),
-        (la, 2), (fa, 0), (s2,), (la, 3), (fa, 2), (lb, 0), (fa, 1), (fa, 3), (lb, 2), (fr,), (dot, 4),
-        (fb, 0), (lb, 1), (lb, 3), (fb, 2), (la, 4), (dot, 6), (s3,), (fa, 4), (la, 6), (dot, 5),
-        (fb, 1), (lb, 4), (nm, 1), (fb, 3), (fa, 6), (dot, 7), (nm, 0), (fb, 4), (lb, 6), (la, 5),
-        (d0,), (nm, 3), (la, 7), (ti, 3), (fb, 6), (nm, 2), (ti, 4), (fa, 5), (ti, 0), (d1,), (fa, 7),
-        (ti, 6), (lb, 5), (f2, 4), (ti, 1), (ti, 2), (d2,), (lb, 7), (f2, 6), (g1, 4), (fb, 5),
-        (fb, 7), (g1, 6), (f2, 2), (d3,), (ti, 5), (f2, 0), (ti, 7), (d4,), (f1, 6), (e0,), (f1, 4),
-        (f2, 7), (f2, 5), (g1, 0), (bk, 6), (e1,), (g1, 7), (g1, 5), (bk, 4), (e2,), (f1, 7), (f2, 1),
-        (f2, 3), (g1, 2), (f1, 5), (f1, 0), (bk, 7), (g1, 3), (g1, 1), (f1, 2), (bk, 5), (f1, 3),
-        (e3,), (bk, 0), (f1, 1), (bk, 2), (bk, 3), (bk, 1), (end,),
+        (raw0,), (dot, 0), (s0,), (dot, 1), (dot, 2), (raw1,), (la, 0), (s1,), (la, 2), (la, 1),
+        (dot, 3), (fa, 2), (fa, 0), (fa, 1), (s2,), (la, 3), (lb, 2), (lb, 0), (lb, 1), (fa, 3), (fr,),
+        (dot, 4), (fb, 0), (lb, 3), (fb, 2), (la, 4), (dot, 6), (s3,), (fb, 3), (fa, 4), (la, 6),
+        (dot, 5), (nm, 0), (fb, 1), (nm, 1), (lb, 4), (fa, 6), (dot, 7), (lb, 6), (fb, 4), (d0,),
+        (la, 5), (nm, 3), (la, 7), (ti, 2), (fb, 6), (nm, 2), (ti, 4), (fa, 5), (ti, 0), (d1,),
+        (fa, 7), (ti, 6), (f2, 4), (lb, 5), (f2, 2), (ti, 3), (lb, 7), (d2,), (f2, 6), (g1, 4),
+        (fb, 5), (g1, 6), (fb, 7), (d3,), (ti, 1), (ti, 5), (ti, 7), (f1, 6), (f2, 0), (f2, 1), (d4,),
+        (f2, 7), (f2, 5), (f2, 3), (f1, 4), (bk, 6), (g1, 7), (e0,), (g1, 5), (bk, 4), (f1, 7), (e1,),
+        (g1, 3), (f1, 5), (g1, 2), (bk, 7), (e2,), (g1, 1), (f1, 3), (g1, 0), (bk, 5), (f1, 2),
+        (f1, 1), (bk, 3), (f1, 0), (e3,), (bk, 2), (bk, 1), (bk, 0), (end,),
     ]
     for step, *args in order:
         step(*args)

time: 121 us -> 121 us (level)
  no operation moved by 1% of the time
where the time goes in v4:
time: 121 us; the launch traced here: 120 us
  Pallas kernels  114 us (94%)
  local copies, waits for them, and re-layouts  5.82 us (5%)
    pallas_call x1, Pallas kernels, shards(): pl.pallas_call(kernel, out_shape=(jax.ShapeDtypeStruct((ROWS, FB), f32),...  114 us
    unnamed x4, local copies, waits for them, and re-layouts  4.63 us

profile of v4, /device:TPU:0, one launch (start us, length us, event | category | flops | bytes accessed | tf_op | source)
XLA Modules:
  0.0 120.4 jit_solution(6146958054850353504)
XLA Ops:
  0.6 114.0 %barlow.1 = (f32[512,1024]{1,0:T(8,128)}, f32[512,1024]{1,0:T(8,128)}, f32[8,128]{1,0:T(8,128)}) custom-call(bf16[512,1024]{1,0:T(8,128)(2,1)} %a_ref.1, bf16[512,1024]{1,0:T(8,128)(2,1)} %b_ref.1), custom_call_target="tpu_custom_call" | custom-call | tf_op jit(solution)/shard_map/barlow/pallas_call | solution.py:563
  114.6 1.2 slice.3
  115.8 0.0 copy-start
  115.8 3.3 %copy.7 = f32[512,1024]{1,0:T(8,128)} copy(f32[512,1024]{1,0:T(8,128)} %get-tuple-element.12) | data formatting | bytes 4194304
  119.1 0.0 copy-done
  119.1 1.3 %copy.8 = f32[512,1024]{1,0:T(8,128)} copy(f32[512,1024]{1,0:T(8,128)S(1)} %copy-done) | data formatting | bytes 4194304
Async XLA Ops:
  115.8 3.3 %copy-start = (f32[512,1024]{1,0:T(8,128)S(1)}, f32[512,1024]{1,0:T(8,128)}, u32[]{:S(2)}) copy-start(f32[512,1024]{1,0:T(8,128)} %get-tuple-element.13) | copy-start | bytes 6291460

commit v5 on v4

--- a/solution.py
+++ b/solution.py
@@ -474,7 +474,8 @@
 
         def finish_a(i, _):
             s = pl.ds(pl.multiple_of(i * 32, 32), 32)
-            ga_ref[s, :] = inv_a * (acc_a[s, :] - c_a - na[s, :].astype(f32) * m_a)
+            ga_ref[s, :] = (
+                inv_a * (acc_a[s, :] - c_a - na[s, :].astype(f32) * m_a)).astype(bf16)
             return 0
 
         lax.fori_loop(0, ROWS // 32, finish_a, 0)
@@ -491,22 +492,23 @@
 
         def finish_b(i, _):
             s = pl.ds(pl.multiple_of(i * 32, 32), 32)
-            gb_ref[s, :] = inv_b * (back_b(s) - c_b - bn[0, s, :].astype(f32) * m_b)
+            gb_ref[s, :] = (
+                inv_b * (back_b(s) - c_b - bn[0, s, :].astype(f32) * m_b)).astype(bf16)
             return 0
 
         lax.fori_loop(0, ROWS // 32, finish_b, 0)
 
     order = [
-        (raw0,), (dot, 0), (s0,), (dot, 1), (dot, 2), (raw1,), (la, 0), (s1,), (la, 2), (la, 1),
-        (dot, 3), (fa, 2), (fa, 0), (fa, 1), (s2,), (la, 3), (lb, 2), (lb, 0), (lb, 1), (fa, 3), (fr,),
-        (dot, 4), (fb, 0), (lb, 3), (fb, 2), (la, 4), (dot, 6), (s3,), (fb, 3), (fa, 4), (la, 6),
-        (dot, 5), (nm, 0), (fb, 1), (nm, 1), (lb, 4), (fa, 6), (dot, 7), (lb, 6), (fb, 4), (d0,),
-        (la, 5), (nm, 3), (la, 7), (ti, 2), (fb, 6), (nm, 2), (ti, 4), (fa, 5), (ti, 0), (d1,),
-        (fa, 7), (ti, 6), (f2, 4), (lb, 5), (f2, 2), (ti, 3), (lb, 7), (d2,), (f2, 6), (g1, 4),
-        (fb, 5), (g1, 6), (fb, 7), (d3,), (ti, 1), (ti, 5), (ti, 7), (f1, 6), (f2, 0), (f2, 1), (d4,),
-        (f2, 7), (f2, 5), (f2, 3), (f1, 4), (bk, 6), (g1, 7), (e0,), (g1, 5), (bk, 4), (f1, 7), (e1,),
-        (g1, 3), (f1, 5), (g1, 2), (bk, 7), (e2,), (g1, 1), (f1, 3), (g1, 0), (bk, 5), (f1, 2),
-        (f1, 1), (bk, 3), (f1, 0), (e3,), (bk, 2), (bk, 1), (bk, 0), (end,),
+        (raw0,), (raw1,), (dot, 0), (s0,), (dot, 1), (la, 0), (dot, 2), (la, 1), (s1,), (dot, 3),
+        (fa, 1), (la, 3), (s2,), (fa, 0), (la, 2), (fa, 3), (lb, 0), (lb, 1), (fa, 2), (lb, 3), (fr,),
+        (dot, 4), (lb, 2), (fb, 1), (fb, 0), (fb, 3), (la, 4), (dot, 6), (s3,), (fa, 4), (la, 6),
+        (dot, 7), (lb, 4), (fb, 2), (nm, 0), (fa, 6), (dot, 5), (nm, 1), (fb, 4), (lb, 6), (la, 7),
+        (nm, 3), (d0,), (nm, 2), (la, 5), (ti, 2), (fb, 6), (ti, 4), (fa, 7), (ti, 3), (d1,), (fa, 5),
+        (ti, 6), (f2, 4), (ti, 1), (lb, 7), (lb, 5), (f2, 2), (d2,), (f2, 6), (g1, 4), (fb, 7),
+        (g1, 6), (fb, 5), (d3,), (ti, 0), (ti, 7), (d4,), (ti, 5), (f1, 6), (f2, 7), (f2, 1), (f1, 4),
+        (f2, 0), (f2, 3), (f2, 5), (bk, 6), (g1, 7), (e0,), (g1, 5), (bk, 4), (f1, 7), (g1, 3), (e1,),
+        (f1, 5), (bk, 7), (g1, 2), (f1, 3), (g1, 1), (g1, 0), (e2,), (bk, 5), (f1, 2), (bk, 3), (e3,),
+        (f1, 1), (f1, 0), (bk, 2), (bk, 1), (bk, 0), (end,),
     ]
     for step, *args in order:
         step(*args)
@@ -563,8 +565,8 @@
     ga, gb, loss = pl.pallas_call(
         kernel,
         out_shape=(
-            jax.ShapeDtypeStruct((ROWS, FB), f32),
-            jax.ShapeDtypeStruct((ROWS, FB), f32),
+            jax.ShapeDtypeStruct((ROWS, FB), bf16),
+            jax.ShapeDtypeStruct((ROWS, FB), bf16),
             jax.ShapeDtypeStruct((8, 128), f32),
         ),
         in_specs=[vm, vm],
@@ -574,7 +576,7 @@
             collective_id=0, has_side_effects=True, vmem_limit_bytes=60 * 2**20),
         name="barlow",
     )(view_a, view_b)
-    return ga, gb, loss[0, 0]
+    return ga.astype(f32), gb.astype(f32), loss[0, 0]
 
 
 def solution(mesh):

time: 121 us -> 119 us (0.983)
  local copies, waits for them, and re-layouts: 5.82 us -> 1.29 us
  other arithmetic: 0 us -> 4.35 us
  Pallas kernels: 114 us -> 112 us
    unnamed x4 -> x2, local copies, waits for them, and re-layouts: 4.63 us -> 0.01 us
    convert_element_type x0 -> x2, other arithmetic: none -> 4.35 us  [shards(): return (ga.astype(f32), gb.astype(f32), loss[0, 0])]
    pallas_call x1, Pallas kernels: 114 us -> 112 us  [shards(): pl.pallas_call(kernel, out_shape=(jax.ShapeDtypeStruct((ROWS, FB), bf16),...]
where the time goes in v5:
time: 119 us
  Pallas kernels  112 us (94%)
  other arithmetic  4.35 us (4%)
  local copies, waits for them, and re-layouts  1.29 us (1%)
    pallas_call x1, Pallas kernels, shards(): pl.pallas_call(kernel, out_shape=(jax.ShapeDtypeStruct((ROWS, FB), bf16),...  112 us
    convert_element_type x2, other arithmetic, shards(): return (ga.astype(f32), gb.astype(f32), loss[0, 0])  4.35 us

profile of v5, /device:TPU:0, one launch (start us, length us, event | category | flops | bytes accessed | tf_op | source)
XLA Modules:
  0.0 118.6 jit_solution(15327203787464454095)
XLA Ops:
  0.6 112.3 %barlow.1 = (bf16[512,1024]{1,0:T(8,128)(2,1)}, bf16[512,1024]{1,0:T(8,128)(2,1)}, f32[8,128]{1,0:T(8,128)}) custom-call(bf16[512,1024]{1,0:T(8,128)(2,1)} %a_ref.1, bf16[512,1024]{1,0:T(8,128)(2,1)} %b_ref.1), custom_call_target="tpu_custom_call" | custom-call | tf_op jit(solution)/shard_map/barlow/pallas_call | solution.py:565
  112.9 0.0 copy-start
  112.9 1.3 %slice.3 = f32[1,1]{1,0:T(1,128)} slice(f32[8,128]{1,0:T(8,128)} %get-tuple-element.8), slice={[0:1], [0:1]} | slice | bytes 8 | tf_op jit(solution)/shard_map/slice | solution.py:579
  114.2 2.8 %convert_element_type.6 = f32[512,1024]{1,0:T(8,128)} convert(bf16[512,1024]{1,0:T(8,128)(2,1)} %get-tuple-element.6) | non-fusion elementwise | flops 524288 | bytes 3145728 | tf_op jit(solution)/shard_map/convert_element_type | solution.py:579
  117.0 0.0 copy-done
  117.0 1.6 %convert_element_type.7 = f32[512,1024]{1,0:T(8,128)} convert(bf16[512,1024]{1,0:T(8,128)(2,1)S(1)} %copy-done) | non-fusion elementwise | flops 524288 | bytes 3145728 | tf_op jit(solution)/shard_map/convert_element_type | solution.py:579
Async XLA Ops:
  112.9 4.1 %copy-start = (bf16[512,1024]{1,0:T(8,128)(2,1)S(1)}, bf16[512,1024]{1,0:T(8,128)(2,1)}, u32[]{:S(2)}) copy-start(bf16[512,1024]{1,0:T(8,128)(2,1)} %get-tuple-element.7) | copy-start | bytes 3145732

commit v6 on v5

--- a/solution.py
+++ b/solution.py
@@ -499,16 +499,16 @@
         lax.fori_loop(0, ROWS // 32, finish_b, 0)
 
     order = [
-        (raw0,), (raw1,), (dot, 0), (s0,), (dot, 1), (la, 0), (dot, 2), (la, 1), (s1,), (dot, 3),
-        (fa, 1), (la, 3), (s2,), (fa, 0), (la, 2), (fa, 3), (lb, 0), (lb, 1), (fa, 2), (lb, 3), (fr,),
-        (dot, 4), (lb, 2), (fb, 1), (fb, 0), (fb, 3), (la, 4), (dot, 6), (s3,), (fa, 4), (la, 6),
-        (dot, 7), (lb, 4), (fb, 2), (nm, 0), (fa, 6), (dot, 5), (nm, 1), (fb, 4), (lb, 6), (la, 7),
-        (nm, 3), (d0,), (nm, 2), (la, 5), (ti, 2), (fb, 6), (ti, 4), (fa, 7), (ti, 3), (d1,), (fa, 5),
-        (ti, 6), (f2, 4), (ti, 1), (lb, 7), (lb, 5), (f2, 2), (d2,), (f2, 6), (g1, 4), (fb, 7),
-        (g1, 6), (fb, 5), (d3,), (ti, 0), (ti, 7), (d4,), (ti, 5), (f1, 6), (f2, 7), (f2, 1), (f1, 4),
-        (f2, 0), (f2, 3), (f2, 5), (bk, 6), (g1, 7), (e0,), (g1, 5), (bk, 4), (f1, 7), (g1, 3), (e1,),
-        (f1, 5), (bk, 7), (g1, 2), (f1, 3), (g1, 1), (g1, 0), (e2,), (bk, 5), (f1, 2), (bk, 3), (e3,),
-        (f1, 1), (f1, 0), (bk, 2), (bk, 1), (bk, 0), (end,),
+        (raw0,), (raw1,), (dot, 0), (s0,), (dot, 1), (dot, 2), (la, 1), (s1,), (la, 2), (la, 0),
+        (dot, 3), (fa, 2), (s2,), (fa, 0), (fa, 1), (la, 3), (lb, 2), (lb, 0), (lb, 1), (fr,),
+        (dot, 4), (fb, 2), (fb, 1), (fa, 3), (fb, 0), (dot, 6), (la, 4), (s3,), (la, 6), (nm, 1),
+        (dot, 7), (nm, 0), (nm, 2), (fa, 6), (fa, 4), (ti, 0), (lb, 3), (d0,), (lb, 6), (la, 7),
+        (lb, 4), (dot, 5), (fb, 6), (f2, 0), (nm, 3), (fb, 4), (fa, 7), (la, 5), (ti, 6), (ti, 1),
+        (lb, 7), (fb, 3), (ti, 4), (fa, 5), (f2, 6), (ti, 2), (d1,), (fb, 7), (f2, 4), (f2, 1),
+        (lb, 5), (g1, 6), (g1, 4), (d2,), (fb, 5), (ti, 7), (f1, 6), (d3,), (f2, 2), (ti, 5), (f2, 7),
+        (f1, 4), (ti, 3), (d4,), (bk, 6), (f2, 5), (g1, 7), (e0,), (f2, 3), (g1, 5), (bk, 4), (f1, 7),
+        (g1, 3), (e1,), (f1, 5), (g1, 2), (bk, 7), (e2,), (g1, 1), (bk, 5), (f1, 3), (g1, 0), (f1, 2),
+        (e3,), (bk, 3), (f1, 1), (f1, 0), (bk, 2), (bk, 1), (bk, 0), (end,),
     ]
     for step, *args in order:
         step(*args)
@@ -522,6 +522,12 @@
         (lo.at[pl.ds(0, 9)], "l"),
     ):
         await_sent(region, name)
+
+
+def widen(a_ref, b_ref, l_ref, ga_ref, gb_ref, loss_ref):
+    ga_ref[...] = a_ref[...].astype(f32)
+    gb_ref[...] = b_ref[...].astype(f32)
+    loss_ref[...] = l_ref[0:1, 0:1]
 
 
 def shards(view_a, view_b):
@@ -576,7 +582,23 @@
             collective_id=0, has_side_effects=True, vmem_limit_bytes=60 * 2**20),
         name="barlow",
     )(view_a, view_b)
-    return ga.astype(f32), gb.astype(f32), loss[0, 0]
+    n = 4
+    block = pl.BlockSpec((ROWS // n, FB), lambda i: (i, 0))
+    one = pl.BlockSpec((1, 1), lambda i: (0, 0))
+    ga, gb, loss = pl.pallas_call(
+        widen,
+        grid=(n,),
+        out_shape=(
+            jax.ShapeDtypeStruct((ROWS, FB), f32),
+            jax.ShapeDtypeStruct((ROWS, FB), f32),
+            jax.ShapeDtypeStruct((1, 1), f32),
+        ),
+        in_specs=[block, block, pl.BlockSpec((8, 128), lambda i: (0, 0))],
+        out_specs=(block, block, one),
+        compiler_params=pltpu.CompilerParams(vmem_limit_bytes=60 * 2**20),
+        name="widen",
+    )(ga, gb, loss)
+    return ga, gb, loss[0, 0]
 
 
 def solution(mesh):

time: 119 us -> 116 us (0.975)
  other arithmetic: 4.35 us -> 0 us
  Pallas kernels: 112 us -> 116 us
  local copies, waits for them, and re-layouts: 1.29 us -> 0 us
    convert_element_type x2 -> x0, other arithmetic: 4.35 us -> none  [shards(): return (ga.astype(f32), gb.astype(f32), loss[0, 0])]
    pallas_call x0 -> x1, Pallas kernels: none -> 4.14 us  [shards(): pl.pallas_call(widen, grid=(n,), out_shape=(jax.ShapeDtypeStruct((ROWS, F...]
    slice x1 -> x0, local copies, waits for them, and re-layouts: 1.28 us -> none  [shards(): return (ga.astype(f32), gb.astype(f32), loss[0, 0])]
where the time goes in v6:
time: 116 us
  Pallas kernels  116 us (100%)
    pallas_call x1, Pallas kernels, shards(): pl.pallas_call(kernel, out_shape=(jax.ShapeDtypeStruct((ROWS, FB), bf16),...  111 us
    pallas_call x1, Pallas kernels, shards(): pl.pallas_call(widen, grid=(n,), out_shape=(jax.ShapeDtypeStruct((ROWS, F...  4.14 us

profile of v6, /device:TPU:0, one launch (start us, length us, event | category | flops | bytes accessed | tf_op | source)
XLA Modules:
  0.0 116.2 jit_solution(12330503057901315917)
XLA Ops:
  0.6 111.4 %barlow.1 = (bf16[512,1024]{1,0:T(8,128)(2,1)}, bf16[512,1024]{1,0:T(8,128)(2,1)}, f32[8,128]{1,0:T(8,128)}) custom-call(bf16[512,1024]{1,0:T(8,128)(2,1)} %a_ref.1, bf16[512,1024]{1,0:T(8,128)(2,1)} %b_ref.1), custom_call_target="tpu_custom_call" | custom-call | tf_op jit(solution)/shard_map/barlow/pallas_call | solution.py:571
  112.1 4.1 %widen.1 = (f32[512,1024]{1,0:T(8,128)}, f32[512,1024]{1,0:T(8,128)}, f32[1,1]{1,0:T(1,128)}) custom-call(bf16[512,1024]{1,0:T(8,128)(2,1)} %get-tuple-element.9.a_ref, bf16[512,1024]{1,0:T(8,128)(2,1)} %get-tuple-element.10.b_ref, f32[8,128]{1,0:T(8,128)} %get-tuple-element.11.l_ref), custom_call_target="tpu_custom_call" | custom-call | tf_op jit(solution)/shard_map/widen/pallas_call | solution.py:588
